TPU v7x, 32 devices: a whole 2x2x4 slice. The times are simulated.
32 devices in a mesh: row: 8 (over z, y), col: 4 (over x, core).
Axes of the slice: x: 2, y: 2, z: 4, core: 2. Of those that a mesh axis runs over, the one named last changes fastest.
Arguments:
- tokens: bfloat16 [8192, 1024], P('row', 'col'), may hold values from -6 to 6
- segment_ids: int32 [8, 1024], P('row'), may hold values from 0 to 7, never falling along the last dimension, each value on 1 to 512 neighbouring positions
- w_query: bfloat16 [1024, 1024], P('row', 'col'), may hold values from -0.1875 to 0.1875
- key_matrix: bfloat16 [1024, 512], P('row', 'col'), may hold values from -0.1875 to 0.1875
- value_matrix: bfloat16 [1024, 512], P('row', 'col'), may hold values from -0.1875 to 0.1875
- w_out: bfloat16 [1024, 1024], P('col', 'row'), may hold values from -0.75 to 0.75
- w_gate: bfloat16 [1024, 4608], P('row', 'col'), may hold values from -0.1875 to 0.1875
- w_up: bfloat16 [1024, 4608], P('row', 'col'), may hold values from -0.1875 to 0.1875
- w_down: bfloat16 [4608, 1024], P('col', 'row'), may hold values from -0.09375 to 0.09375
- norm_attn: float32 [1024], replicated, may hold values from 0.1 to 1.9
- norm_ffn: float32 [1024], replicated, may hold values from 0.1 to 1.9
- norm_query: float32 [64], replicated, may hold values from 0.1 to 1.9
- norm_key: float32 [64], replicated, may hold values from 0.1 to 1.9
- cotangent: bfloat16 [8192, 1024], P('row', 'col'), may hold values from -6 to 6
Outputs:
- layer_out: bfloat16 [8192, 1024], P('row', 'col')
- grad_tokens: float32 [8192, 1024], P('row', 'col')
- grad_w_query: float32 [1024, 1024], P('row', 'col')
- grad_w_key: float32 [1024, 512], P('row', 'col')
- grad_w_value: float32 [1024, 512], P('row', 'col')
- grad_w_out: float32 [1024, 1024], P('col', 'row')
- grad_w_gate: float32 [1024, 4608], P('row', 'col')
- grad_w_up: float32 [1024, 4608], P('row', 'col')
- grad_w_down: float32 [4608, 1024], P('col', 'row')
- grad_norm_attn: float32 [1024], replicated
- grad_norm_ffn: float32 [1024], replicated
- grad_norm_query: float32 [64], replicated
- grad_norm_key: float32 [64], replicated
Inputs may be any that keep to these rules, and one draw needn't show every extreme that they name: `segment_ids`: within each sequence the ids never fall, and a document spans at most 512 tokens.
All inputs are finite; a program needn't handle non-finite values.
Results may differ from a plain program's by a relative error of at most 0.012.
The roundings to bfloat16 on the way count: a program that leaves them out, or rounds other values in their place, can miss the bound.
Values may be sent and summed in bfloat16 or wider, within the bound.
A program may use at most 192 MiB of HBM per device.

v0:
```python
import functools
import math

import jax
import jax.numpy as jnp
from jax import lax
from jax.sharding import PartitionSpec as P

epsilon = 1e-05
rope_base = 1000000.0


def root_norm(operand):
    return operand * lax.rsqrt(jnp.mean(operand * operand, axis=-1, keepdims=True) + epsilon)


def gain_norm(operand, gain):
    return root_norm(operand) * gain


def swish_product(gate_in, up_in):
    return jax.nn.silu(gate_in) * up_in


def doc_positions(segment_row):
    token_length = segment_row.shape[0]
    places = jnp.arange(token_length, dtype=jnp.int32)
    doc_starts = jnp.concatenate([jnp.ones((1,), dtype=bool), segment_row[1:] != segment_row[:-1]])
    first_place = lax.cummax(jnp.where(doc_starts, places, 0), axis=0)
    return places - first_place


def rotate(operand, positions):
    half_size = operand.shape[-1] // 2
    freq_steps = jnp.arange(half_size, dtype=jnp.float32) * (2.0 / operand.shape[-1])
    inverse_freq = jnp.exp(-freq_steps * math.log(rope_base))
    angles = positions.astype(jnp.float32)[:, None] * inverse_freq[None, :]
    cosine = jnp.cos(angles)[:, None, :]
    sine_val = jnp.sin(angles)[:, None, :]
    front_half = operand[..., :half_size]
    back_half = operand[..., half_size:]
    return jnp.concatenate(
        [front_half * cosine - back_half * sine_val, back_half * cosine + front_half * sine_val],
        axis=-1,
    )


def head_prep(query_pre, key_before_rotation, gain_query, gain_key, positions, head_size):
    token_length = query_pre.shape[0]
    query_head_rows = query_pre.reshape(token_length, -1, head_size)
    key_heads = key_before_rotation.reshape(token_length, -1, head_size)
    return (
        rotate(root_norm(query_head_rows) * gain_query, positions),
        rotate(root_norm(key_heads) * gain_key, positions),
    )


def plain_dot(left_mat, right_mat):
    return jnp.dot(left_mat, right_mat, preferred_element_type=jnp.float32)


def lead_dot(left_mat, right_mat):
    return lax.dot_general(
        left_mat, right_mat, (((0,), (0,)), ((), ())), preferred_element_type=jnp.float32
    )


def tail_dot(left_mat, right_mat):
    return lax.dot_general(
        left_mat, right_mat, (((1,), (1,)), ((), ())), preferred_element_type=jnp.float32
    )


def block_mask(segment_row, start_row, stop_row):
    places = jnp.arange(stop_row, dtype=jnp.int32)
    same_doc = segment_row[start_row:stop_row, None] == segment_row[None, :stop_row]
    return same_doc & (places[None, :] <= places[start_row:stop_row, None])


def attend_forward(query_head_rows, key_heads, value_head_rows, segment_row, block_rows):
    token_length = query_head_rows.shape[0]
    score_scale = query_head_rows.shape[-1] ** (-0.5)
    outputs, row_tops, row_totals = ([], [], [])
    for start_row in range(0, token_length, block_rows):
        stop_row = start_row + block_rows
        allowed = block_mask(segment_row, start_row, stop_row)
        raw_scores = jnp.einsum(
            "qhgd,khd->hgqk",
            query_head_rows[start_row:stop_row],
            key_heads[:stop_row],
            preferred_element_type=jnp.float32,
        )
        masked = jnp.where(allowed, raw_scores * score_scale, -1e30)
        row_top = jnp.max(masked, axis=-1, keepdims=True)
        exponent = jnp.exp(masked - row_top)
        row_total = jnp.sum(exponent, axis=-1, keepdims=True)
        weights = (exponent / row_total).astype(jnp.bfloat16)
        outputs.append(
            jnp.einsum(
                "hgqk,khd->qhgd",
                weights,
                value_head_rows[:stop_row],
                preferred_element_type=jnp.float32,
            )
        )
        row_tops.append(row_top)
        row_totals.append(row_total)
    return (jnp.concatenate(outputs, axis=0), row_tops, row_totals)


def attend_backward(
    query_head_rows,
    key_heads,
    value_head_rows,
    grad_mixed,
    segment_row,
    block_rows,
    row_tops,
    row_totals,
):
    token_length = query_head_rows.shape[0]
    score_scale = query_head_rows.shape[-1] ** (-0.5)
    grad_query = []
    grad_keys = jnp.zeros(key_heads.shape, jnp.float32)
    grad_values = jnp.zeros(value_head_rows.shape, jnp.float32)
    for block_index, start_row in enumerate(range(0, token_length, block_rows)):
        stop_row = start_row + block_rows
        allowed = block_mask(segment_row, start_row, stop_row)
        raw_scores = jnp.einsum(
            "qhgd,khd->hgqk",
            query_head_rows[start_row:stop_row],
            key_heads[:stop_row],
            preferred_element_type=jnp.float32,
        )
        masked = jnp.where(allowed, raw_scores * score_scale, -1e30)
        prob_vals = jnp.exp(masked - row_tops[block_index]) / row_totals[block_index]
        weights = prob_vals.astype(jnp.bfloat16)
        grad_probs = jnp.einsum(
            "qhgd,khd->hgqk",
            grad_mixed[start_row:stop_row],
            value_head_rows[:stop_row],
            preferred_element_type=jnp.float32,
        )
        inner_sum = jnp.sum(prob_vals * grad_probs, axis=-1, keepdims=True)
        grad_scores = (prob_vals * (grad_probs - inner_sum)).astype(jnp.bfloat16)
        grad_query.append(
            jnp.einsum(
                "hgqk,khd->qhgd",
                grad_scores,
                key_heads[:stop_row],
                preferred_element_type=jnp.float32,
            )
            * score_scale
        )
        padding = ((0, token_length - stop_row), (0, 0), (0, 0))
        key_term = (
            jnp.einsum(
                "hgqk,qhgd->khd",
                grad_scores,
                query_head_rows[start_row:stop_row],
                preferred_element_type=jnp.float32,
            )
            * score_scale
        )
        value_term = jnp.einsum(
            "hgqk,qhgd->khd",
            weights,
            grad_mixed[start_row:stop_row],
            preferred_element_type=jnp.float32,
        )
        grad_keys = grad_keys + jnp.pad(key_term, padding)
        grad_values = grad_values + jnp.pad(value_term, padding)
    return (jnp.concatenate(grad_query, axis=0), grad_keys, grad_values)


def per_device(
    tokens,
    segment_ids,
    w_query,
    key_matrix,
    value_matrix,
    w_out,
    w_gate,
    w_up,
    w_down,
    norm_attn,
    norm_ffn,
    norm_query,
    norm_key,
    cotangent,
):
    column = lax.axis_index("col")
    part_width = tokens.shape[1]
    token_length = tokens.shape[0]
    head_size = norm_query.shape[0]
    segment_row = segment_ids[0]
    positions = doc_positions(segment_row)
    block_rows = min(512, token_length)
    offset = column * part_width
    gathered = lax.all_gather(tokens, "col", axis=1, tiled=True).astype(jnp.float32)
    full_width = gathered.shape[1]
    own_mask = (jnp.arange(full_width, dtype=jnp.int32) // part_width == column).astype(jnp.float32)
    full_query, full_key, full_value, full_out = (
        lax.all_gather(w_query, "row", axis=0, tiled=True),
        lax.all_gather(key_matrix, "row", axis=0, tiled=True),
        lax.all_gather(value_matrix, "row", axis=0, tiled=True),
        lax.all_gather(w_out, "row", axis=1, tiled=True),
    )
    normalized_input, norm_attn_back = jax.vjp(gain_norm, gathered, norm_attn)
    normed_low = normalized_input.astype(jnp.bfloat16)
    query_pre = plain_dot(normed_low, full_query)
    key_before_rotation = plain_dot(normed_low, full_key)
    value_pre = plain_dot(normed_low, full_value)
    prep_fn = functools.partial(head_prep, positions=positions, head_size=head_size)
    rotated, prep_back = jax.vjp(prep_fn, query_pre, key_before_rotation, norm_query, norm_key)
    query_rot, key_rot = rotated
    kv_local = key_rot.shape[1]
    heads_per_group = query_rot.shape[1] // kv_local
    query_low = query_rot.astype(jnp.bfloat16).reshape(
        token_length, kv_local, heads_per_group, head_size
    )
    key_low = key_rot.astype(jnp.bfloat16)
    value_low = value_pre.astype(jnp.bfloat16).reshape(token_length, kv_local, head_size)
    mixed_out, row_tops, row_totals = attend_forward(
        query_low, key_low, value_low, segment_row, block_rows
    )
    mixed_low = mixed_out.reshape(token_length, -1).astype(jnp.bfloat16)
    attn_partial = plain_dot(mixed_low, full_out)
    attended = lax.psum(attn_partial, "col")
    residual = gathered + attended
    normed_ffn, norm_ffn_back = jax.vjp(gain_norm, residual, norm_ffn)
    ffn_low = normed_ffn.astype(jnp.bfloat16)
    residual_mine = lax.dynamic_slice_in_dim(residual, offset, part_width, 1)
    full_gate, full_up, full_down = (
        lax.all_gather(w_gate, "row", axis=0, tiled=True),
        lax.all_gather(w_up, "row", axis=0, tiled=True),
        lax.all_gather(w_down, "row", axis=1, tiled=True),
    )
    gate_act = plain_dot(ffn_low, full_gate)
    up_act = plain_dot(ffn_low, full_up)
    hidden, swish_back = jax.vjp(swish_product, gate_act, up_act)
    hidden_low = hidden.astype(jnp.bfloat16)
    branch = lax.psum_scatter(
        plain_dot(hidden_low, full_down).astype(jnp.bfloat16),
        "col",
        scatter_dimension=1,
        tiled=True,
    ).astype(jnp.float32)
    layer_out = (residual_mine + branch).astype(jnp.bfloat16)
    grad_whole = lax.all_gather(cotangent, "col", axis=1, tiled=True)
    grad_down_w = lead_dot(hidden_low, grad_whole)
    grad_hidden = tail_dot(grad_whole, full_down)
    grad_gate, grad_up = swish_back(grad_hidden)
    gate_low = grad_gate.astype(jnp.bfloat16)
    up_low = grad_up.astype(jnp.bfloat16)
    grad_gate_w = lead_dot(ffn_low, gate_low)
    grad_up_w = lead_dot(ffn_low, up_low)
    ffn_norm_partial = tail_dot(gate_low, full_gate) + tail_dot(up_low, full_up)
    grad_normed_ffn = lax.psum(ffn_norm_partial, "col")
    grad_residual, grad_gain_ffn = norm_ffn_back(grad_normed_ffn)
    grad_residual = grad_residual + grad_whole.astype(jnp.float32)
    residual_low = grad_residual.astype(jnp.bfloat16)
    residual_grad_mine = lax.dynamic_slice_in_dim(grad_residual, offset, part_width, 1)
    ffn_gain_term = grad_gain_ffn * own_mask
    grad_out_w = lead_dot(mixed_low, residual_low)
    grad_mixed = (
        tail_dot(residual_low, full_out)
        .astype(jnp.bfloat16)
        .reshape(token_length, kv_local, heads_per_group, head_size)
    )
    grad_query, grad_keys, grad_values = attend_backward(
        query_low, key_low, value_low, grad_mixed, segment_row, block_rows, row_tops, row_totals
    )
    grad_query_pre, grad_key_pre, grad_gain_query, grad_gain_key = prep_back(
        (grad_query.reshape(token_length, -1, head_size), grad_keys)
    )
    query_grad_low = grad_query_pre.astype(jnp.bfloat16)
    key_grad_low = grad_key_pre.astype(jnp.bfloat16)
    value_grad_low = grad_values.reshape(token_length, -1).astype(jnp.bfloat16)
    grad_query_w = lead_dot(normed_low, query_grad_low)
    grad_key_w = lead_dot(normed_low, key_grad_low)
    grad_value_w = lead_dot(normed_low, value_grad_low)
    grad_normed_part = (
        tail_dot(query_grad_low, full_query)
        + tail_dot(key_grad_low, full_key)
        + tail_dot(value_grad_low, full_value)
    )
    grad_normed = lax.psum(grad_normed_part, "col")
    grad_input, grad_gain_attn = norm_attn_back(grad_normed)
    grad_tokens = lax.dynamic_slice_in_dim(grad_input, offset, part_width, 1) + residual_grad_mine
    attn_gain_term = grad_gain_attn * own_mask
    attn_grads = (
        lax.psum_scatter(grad_query_w, "row", scatter_dimension=0, tiled=True),
        lax.psum_scatter(grad_key_w, "row", scatter_dimension=0, tiled=True),
        lax.psum_scatter(grad_value_w, "row", scatter_dimension=0, tiled=True),
        lax.psum_scatter(grad_out_w, "row", scatter_dimension=1, tiled=True),
    )
    ffn_grads = (
        lax.psum_scatter(grad_gate_w, "row", scatter_dimension=0, tiled=True),
        lax.psum_scatter(grad_up_w, "row", scatter_dimension=0, tiled=True),
        lax.psum_scatter(grad_down_w, "row", scatter_dimension=1, tiled=True),
    )
    gain_sums = lax.psum(
        (attn_gain_term, ffn_gain_term, grad_gain_query, grad_gain_key), ("row", "col")
    )
    return (
        layer_out,
        grad_tokens,
        attn_grads[0],
        attn_grads[1],
        attn_grads[2],
        attn_grads[3],
        ffn_grads[0],
        ffn_grads[1],
        ffn_grads[2],
        gain_sums[0],
        gain_sums[1],
        gain_sums[2],
        gain_sums[3],
    )


def solution(mesh):
    in_specs = (
        P("row", "col"),
        P("row", None),
        P("row", "col"),
        P("row", "col"),
        P("row", "col"),
        P("col", "row"),
        P("row", "col"),
        P("row", "col"),
        P("col", "row"),
        P(),
        P(),
        P(),
        P(),
        P("row", "col"),
    )
    out_specs = (
        P("row", "col"),
        P("row", "col"),
        P("row", "col"),
        P("row", "col"),
        P("row", "col"),
        P("col", "row"),
        P("row", "col"),
        P("row", "col"),
        P("col", "row"),
        P(),
        P(),
        P(),
        P(),
    )
    return jax.shard_map(
        per_device, mesh=mesh, in_specs=in_specs, out_specs=out_specs, check_vma=False
    )
```

profile of v0, /device:TPU:0, one launch (start us, length us, event | category | flops | bytes accessed | tf_op | source)
XLA Modules:
  0.0 1157.7 jit_solution(11284256195905428101)
XLA Ops:
  10.3 34.8 %all_gather.29 = bf16[1024,128]{1,0:T(8,128)(2,1)} all-gather(bf16[128,128]{1,0:T(8,128)(2,1)} %param.17), channel_id=1, replica_groups=mesh['row'=8,'col'=4] {'row'}, dimensions={0}, use_global_device_ids=true | all-gather | bytes 294912 | tf_op jit(solution)/shard_map/all_gather | solution.py:205
  45.1 33.0 %all_gather.28 = bf16[1024,128]{1,0:T(8,128)(2,1)} all-gather(bf16[128,128]{1,0:T(8,128)(2,1)} %param.18), channel_id=1, replica_groups=mesh['row'=8,'col'=4] {'row'}, dimensions={0}, use_global_device_ids=true | all-gather | bytes 294912 | tf_op jit(solution)/shard_map/all_gather | solution.py:206
  78.9 33.9 %all_gather.30 = bf16[1024,256]{1,0:T(8,128)(2,1)} all-gather(bf16[128,256]{1,0:T(8,128)(2,1)} %param.16), channel_id=1, replica_groups=mesh['row'=8,'col'=4] {'row'}, dimensions={0}, use_global_device_ids=true | all-gather | bytes 589824 | tf_op jit(solution)/shard_map/all_gather | solution.py:204
  112.9 28.3 %all_gather.31 = bf16[256,1024]{1,0:T(8,128)(2,1)} all-gather(bf16[256,128]{1,0:T(8,128)(2,1)} %param.19), channel_id=1, replica_groups=mesh['row'=8,'col'=4] {'row'}, dimensions={1}, use_global_device_ids=true | all-gather | bytes 589824 | tf_op jit(solution)/shard_map/all_gather | solution.py:207
  142.6 1.9 fusion.24
  144.6 2.1 multiply_reduce_fusion.5
  147.3 2.2 multiply_convert_fusion.3
  155.3 5.4 fusion.104
  160.7 8.1 fusion.99
  168.8 2.8 fusion.48
  171.7 1.9 copy-done.7
  175.2 2.7 fusion.109
  180.7 82.0 %all-reduce.11.cloned.1.call-done = f32[1024,1024]{1,0:T(8,128)} async-done(((f32[1024,1024]{1,0:T(8,128)}), f32[1024,1024]{1,0:T(8,128)}) %all-reduce.11.cloned.1.call-update) | async-done | bytes 4194320 | tf_op jit(solution)/shard_map/psum | solution.py:229
  262.8 3.5 multiply_reduce_fusion.4
  268.3 1.7 multiply_convert_fusion.2
  270.0 7.4 fusion.110
  277.4 7.0 all-gather.10.cloned.1.call-done
  284.4 7.3 fusion.111
  291.7 15.5 %all-gather.14.cloned.1.call-done = bf16[1024,1024]{1,0:T(8,128)(2,1)} async-done(((bf16[1024,256]{1,0:T(8,128)(2,1)}), bf16[1024,1024]{1,0:T(8,128)(2,1)}) %all-gather.14.cloned.1.call-update) | async-done | bytes 2097168 | tf_op jit(solution)/shard_map/all_gather | solution.py:250
  307.1 56.0 %all-gather.12.cloned.1.call-done = bf16[1152,1024]{1,0:T(8,128)(2,1)} async-done(((bf16[1152,128]{1,0:T(8,128)(2,1)}), bf16[1152,1024]{1,0:T(8,128)(2,1)}) %all-gather.12.cloned.1.call-update) | async-done | bytes 2359312 | tf_op jit(solution)/shard_map/all_gather | solution.py:237
  363.1 10.9 multiply_convert_fusion
  374.0 2.9 fusion.112
  377.3 4.5 convolution_add_fusion
  381.9 10.5 reduce-scatter.9.cloned.1.call-start
  392.4 6.6 convolution_convert_fusion
  399.0 66.7 %all-reduce.13.cloned.1.call-done = f32[1024,1024]{1,0:T(8,128)} async-done(((f32[1024,1024]{1,0:T(8,128)}), f32[1024,1024]{1,0:T(8,128)}) %all-reduce.13.cloned.1.call-update) | async-done | bytes 4194320 | tf_op jit(solution)/shard_map/psum | solution.py:259
  465.7 5.2 multiply_reduce_fusion
  471.7 2.7 fusion.10
  481.5 2.4 fusion.4
  492.2 2.7 add_add_fusion.1
  498.4 1.8 fusion.115
  500.2 4.0 fusion.51
  504.4 6.3 fusion.118
  510.7 6.3 fusion.119
  518.6 6.1 fusion.120
  526.4 2.4 convert_element_type.89
  528.8 2.3 add_convert_fusion
  531.1 56.4 %all-reduce.15.cloned.1.call-done = f32[1024,1024]{1,0:T(8,128)} async-done(((f32[1024,1024]{1,0:T(8,128)}), f32[1024,1024]{1,0:T(8,128)}) %all-reduce.15.cloned.1.call-update) | async-done | bytes 4194320 | tf_op jit(solution)/shard_map/psum | solution.py:288
  587.5 5.5 multiply_reduce_fusion.1
  593.0 39.8 %all-reduce.6 = (f32[1024]{0:T(1024)}, f32[1024]{0:T(1024)}, f32[64]{0:T(128)}, f32[64]{0:T(128)}) all-reduce(f32[1024]{0:T(1024)S(1)} %get-tuple-element.60, f32[1024]{0:T(1024)S(1)} %get-tuple-element.59, f32[64]{0:T(128)S(1)} %get-tuple-element.17, f32[64]{0:T(128)S(1)} %get-tuple-element.19), channel_id=1, replica_groups=mesh['row'=8,'col'=4] {'row','col'}, use_global_device_ids=true, to_apply=%region_28.29 | all-reduce | flops 2176 | bytes 17408 | tf_op jit(solution)/shard_map/psum | solution.py:303
  632.8 3.2 fusion.50
  636.0 17.4 %reduce-scatter.15.cloned.1.call-done = f32[128,128]{1,0:T(8,128)} async-done(((f32[1024,128]{1,0:T(8,128)}), f32[128,128]{1,0:T(8,128)}) %reduce-scatter.15.cloned.1.call-update) | async-done | bytes 65552 | tf_op jit(solution)/shard_map/reduce_scatter | solution.py:295
  653.4 65.4 %reduce-scatter.13.cloned.1.call-done = f32[128,128]{1,0:T(8,128)} async-done(((f32[1024,128]{1,0:T(8,128)}), f32[128,128]{1,0:T(8,128)}) %reduce-scatter.13.cloned.1.call-update) | async-done | bytes 65552 | tf_op jit(solution)/shard_map/reduce_scatter | solution.py:294
  718.7 66.5 %reduce-scatter.11.cloned.1.call-done = f32[128,256]{1,0:T(8,128)} async-done(((f32[1024,256]{1,0:T(8,128)}), f32[128,256]{1,0:T(8,128)}) %reduce-scatter.11.cloned.1.call-update) | async-done | bytes 131088 | tf_op jit(solution)/shard_map/reduce_scatter | solution.py:293
  785.2 67.3 %reduce-scatter.17.cloned.1.call-done = f32[256,128]{1,0:T(8,128)} async-done(((f32[256,1024]{1,0:T(8,128)}), f32[256,128]{1,0:T(8,128)}) %reduce-scatter.17.cloned.1.call-update) | async-done | bytes 131088 | tf_op jit(solution)/shard_map/reduce_scatter | solution.py:296
  852.5 98.4 %reduce-scatter.19.cloned.1.call-done = f32[128,1152]{1,0:T(8,128)} async-done(((f32[1024,1152]{1,0:T(8,128)}), f32[128,1152]{1,0:T(8,128)}) %reduce-scatter.19.cloned.1.call-update) | async-done | bytes 589840 | tf_op jit(solution)/shard_map/reduce_scatter | solution.py:299
  950.9 99.3 %reduce-scatter.21.cloned.1.call-done = f32[128,1152]{1,0:T(8,128)} async-done(((f32[1024,1152]{1,0:T(8,128)}), f32[128,1152]{1,0:T(8,128)}) %reduce-scatter.21.cloned.1.call-update) | async-done | bytes 589840 | tf_op jit(solution)/shard_map/reduce_scatter | solution.py:300
  1050.1 99.6 %reduce-scatter.23.cloned.1.call-done = f32[1152,128]{1,0:T(8,128)} async-done(((f32[1152,1024]{1,0:T(8,128)}), f32[1152,128]{1,0:T(8,128)}) %reduce-scatter.23.cloned.1.call-update) | async-done | bytes 589840 | tf_op jit(solution)/shard_map/reduce_scatter | solution.py:301
  (213 shorter events, 40.4 us)
Async XLA Ops:
  8.0 139.3 %copy-start.46 = (f32[1024]{0:T(1024)S(1)}, f32[1024]{0:T(1024)}, u32[]{:S(2)}) copy-start(f32[1024]{0:T(1024)} %param.23) | copy-start | bytes 12292
  8.0 136.6 %all-gather.6.cloned.1.call-start = ((), (), s32[]{:S(2)}) async-start(), calls=%async_computation.8 | async-start | bytes 2621440 | tf_op jit(solution)/shard_map/all_gather | solution.py:200
  8.8 254.0 %all-reduce.11.cloned.1.call-start = ((), (), s32[]{:S(2)}) async-start(), calls=%async_computation.9 | async-start | bytes 8388608 | tf_op jit(solution)/shard_map/psum | solution.py:229
  144.6 4.9 copy-start.10
  147.3 3.0 copy-start.19
  147.3 3.9 copy-start.36
  150.4 2.5 copy-start.17
  151.2 2.5 copy-start.5
  168.8 4.7 copy-start.7
  168.8 4.7 copy-start.27
  168.8 4.7 copy-start.50
  178.0 92.1 %all-gather.8.cloned.1.call-start = ((), (), s32[]{:S(2)}) async-start(), calls=%async_computation.10 | async-start | bytes 2654208 | tf_op jit(solution)/shard_map/all_gather | solution.py:235
  178.5 105.9 %all-gather.10.cloned.1.call-start = ((), (), s32[]{:S(2)}) async-start(), calls=%async_computation.11 | async-start | bytes 2654208 | tf_op jit(solution)/shard_map/all_gather | solution.py:236
  179.1 128.0 %all-gather.14.cloned.1.call-start = ((), (), s32[]{:S(2)}) async-start(), calls=%async_computation.14 | async-start | bytes 2621440 | tf_op jit(solution)/shard_map/all_gather | solution.py:250
  179.7 183.4 %all-gather.12.cloned.1.call-start = ((), (), s32[]{:S(2)}) async-start(), calls=%async_computation.12 | async-start | bytes 2654208 | tf_op jit(solution)/shard_map/all_gather | solution.py:237
  180.4 285.2 %all-reduce.13.cloned.1.call-start = ((), (), s32[]{:S(2)}) async-start(), calls=%async_computation.15 | async-start | bytes 8388608 | tf_op jit(solution)/shard_map/psum | solution.py:259
  262.8 5.5 copy-start.44
  266.3 2.0 copy-start
  363.1 10.9 copy-start.56
  374.0 2.9 copy-start.59
  374.0 2.9 copy-start.58
  374.0 3.4 copy-start.57
  381.9 146.9 %reduce-scatter.9.cloned.1.call-start = ((), (), s32[]{:S(2)}) async-start(), calls=%async_computation.13 | async-start | bytes 2621440 | tf_op jit(solution)/shard_map/reduce_scatter | solution.py:243
  399.0 188.5 %all-reduce.15.cloned.1.call-start = ((), (), s32[]{:S(2)}) async-start(), calls=%async_computation.16 | async-start | bytes 8388608 | tf_op jit(solution)/shard_map/psum | solution.py:288
  465.7 5.2 copy-start.43
  465.7 5.2 copy-start.1
  465.7 6.0 copy-start.4
  465.7 6.0 copy-start.39
  465.7 6.0 copy-start.45
  471.7 2.7 copy-start.13
  471.7 3.5 copy-start.16
  474.4 2.3 copy-start.3
  474.4 5.3 slice-start
  475.5 4.2 slice-start.1
  476.6 2.6 copy-start.23
  494.9 3.5 copy-start.15
  494.9 158.5 %reduce-scatter.15.cloned.1.call-start = ((), (), s32[]{:S(2)}) async-start(), calls=%async_computation.19 | async-start | bytes 589824 | tf_op jit(solution)/shard_map/reduce_scatter | solution.py:295
  496.7 222.0 %reduce-scatter.13.cloned.1.call-start = ((), (), s32[]{:S(2)}) async-start(), calls=%async_computation.18 | async-start | bytes 589824 | tf_op jit(solution)/shard_map/reduce_scatter | solution.py:294
  498.3 286.9 %reduce-scatter.11.cloned.1.call-start = ((), (), s32[]{:S(2)}) async-start(), calls=%async_computation.17 | async-start | bytes 1179648 | tf_op jit(solution)/shard_map/reduce_scatter | solution.py:293
  500.2 4.2 copy-start.21
  500.2 352.3 %reduce-scatter.17.cloned.1.call-start = ((), (), s32[]{:S(2)}) async-start(), calls=%async_computation.20 | async-start | bytes 1179648 | tf_op jit(solution)/shard_map/reduce_scatter | solution.py:296
  504.3 446.6 %reduce-scatter.19.cloned.1.call-start = ((), (), s32[]{:S(2)}) async-start(), calls=%async_computation.21 | async-start | bytes 5308416 | tf_op jit(solution)/shard_map/reduce_scatter | solution.py:299
  510.7 539.4 %reduce-scatter.21.cloned.1.call-start = ((), (), s32[]{:S(2)}) async-start(), calls=%async_computation.22 | async-start | bytes 5308416 | tf_op jit(solution)/shard_map/reduce_scatter | solution.py:300
  517.1 632.6 %reduce-scatter.23.cloned.1.call-start = ((), (), s32[]{:S(2)}) async-start(), calls=%async_computation.23 | async-start | bytes 5308416 | tf_op jit(solution)/shard_map/reduce_scatter | solution.py:301
  526.4 61.2 %copy-start.37 = (f32[1024]{0:T(1024)S(1)}, f32[1024]{0:T(1024)}, u32[]{:S(2)}) copy-start(f32[1024]{0:T(1024)} %copy-done.36) | copy-start | bytes 12292
  526.4 61.2 %copy-start.47 = (f32[1024]{0:T(1024)S(1)}, f32[1024]{0:T(1024)}, u32[]{:S(2)}) copy-start(f32[1024]{0:T(1024)} %param.23) | copy-start | bytes 12292
  531.1 61.9 %copy-start.48 = (f32[1024]{0:T(1024)S(1)}, f32[1024]{0:T(1024)}, u32[]{:S(2)}) copy-start(f32[1024]{0:T(1024)} %get-tuple-element.13) | copy-start | bytes 12292
  531.1 101.7 %copy-start.41 = (f32[1024]{0:T(1024)S(1)}, f32[1024]{0:T(1024)}, u32[]{:S(2)}) copy-start(f32[1024]{0:T(1024)} %copy-done.40) | copy-start | bytes 12292
  (30 other events, 38.9 us)
Sparse Core Ops, SparseCore 0:
  10.4 25.5 all-gather.5
  178.1 84.6 all-reduce.10
  382.0 83.6 all-reduce.12
  468.1 31.5 reduce-scatter.8
  502.0 85.4 all-reduce.14
  591.3 62.0 reduce-scatter.14
  657.7 61.0 reduce-scatter.12
  722.7 62.4 reduce-scatter.10
  789.6 62.8 reduce-scatter.16
  856.6 94.2 reduce-scatter.18
  955.1 94.9 reduce-scatter.20
  1054.2 95.4 reduce-scatter.22
Sparse Core Ops, SparseCore 1:
  180.9 50.9 all-gather.7
  234.1 50.3 all-gather.9
  285.9 21.2 all-gather.13
  309.4 53.6 all-gather.11
where the time goes:
time: 1170 us; the launch traced here: 1160 us
  waiting for transfers between devices  800 us (68%)
  blocking collectives  170 us (15%)
  matrix products  102 us (9%)
  other arithmetic  42.6 us (4%)
  between operations  17 us (1%)
  local copies, waits for them, and re-layouts  13.9 us (1%)
    reduce_scatter x1, waiting for transfers between devices, per_device(): lax.psum_scatter(grad_down_w, 'row', scatter_dimension=1, tiled=True)  99.6 us
    reduce_scatter x1, waiting for transfers between devices, per_device(): lax.psum_scatter(grad_up_w, 'row', scatter_dimension=0, tiled=True)  99.3 us
    reduce_scatter x1, waiting for transfers between devices, per_device(): lax.psum_scatter(grad_gate_w, 'row', scatter_dimension=0, tiled=True)  98.4 us
    psum x1, waiting for transfers between devices, per_device(): attended = lax.psum(attn_partial, 'col')  82 us
    reduce_scatter x1, waiting for transfers between devices, per_device(): lax.psum_scatter(grad_out_w, 'row', scatter_dimension=1, tiled=True)  67.3 us
    psum x1, waiting for transfers between devices, per_device(): grad_normed_ffn = lax.psum(ffn_norm_partial, 'col')  66.7 us
    reduce_scatter x1, waiting for transfers between devices, per_device(): lax.psum_scatter(grad_query_w, 'row', scatter_dimension=0, tiled=True)  66.5 us
    reduce_scatter x1, waiting for transfers between devices, per_device(): lax.psum_scatter(grad_key_w, 'row', scatter_dimension=0, tiled=True)  65.4 us
  transfers between devices with their start and end apart: 16, of which 13 were waited for; matrix products, arithmetic and copies ran while one was open for 9% of the time, Pallas kernels for 0%

commit v1 on v0

v1 whole, which is shorter than its diff:
```python
import functools
import math

import jax
import jax.numpy as jnp
from jax import lax
from jax.experimental import pallas as pl
from jax.experimental.pallas import tpu as pltpu
from jax.sharding import PartitionSpec as P

epsilon = 1e-05
rope_base = 1000000.0
longest = 512
ids = 8
f32, bf16 = jnp.float32, jnp.bfloat16
MESH = pl.DeviceIdType.MESH
RB = 256


def dot_nn(a, b):
    return lax.dot_general(a, b, (((1,), (0,)), ((), ())), preferred_element_type=f32)


def dot_nt(a, b):
    return lax.dot_general(a, b, (((1,), (1,)), ((), ())), preferred_element_type=f32)


def rows(i, n):
    return pl.ds(pl.multiple_of(i * n, n), n)


def layer_kernel(
    nz,
    tok_h, seg_ref, wq_h, wk_h, wv_h, wot_h, wg_h, wu_h, wdt_h, ga_ref, gf_ref, gq_ref, gk_ref, cot_h,
    lo_h, gt_h, gattn_h, ggate_h, gup_h, gdown_h, gain_ref,
    W, G, RY, RZ, GF, Tk, Ct, Nm, R1, PRE, QS, KS, VS, KT, VT, DO, MX, PB, A0, B0, S0, RES, NF, GG, HID,
    CS, SN, BIAS, INV, DQ, DK, DV, AC, BC, SC, LO, LOC, VEC, VC, VX, VY, VZ,
    loc_sem, agz_s, agz_r, agy_s, agy_r, rsy_s, rsy_r, rsz_s, rsz_r,
    cag_s, cag_r, crs_s, crs_r, gn_s, gn_r, lo_s, lo_r, vec_s, vec_r, vz_s, vz_r, out_sem,
):
    T, D = Tk.shape
    br = RY.shape[1]
    QW, KW = PRE.shape[1] // 2, PRE.shape[1] // 4
    PW = 2 * QW + 2 * KW
    F = HID.shape[1]
    FC = F // 3
    nb = T // RB
    CW = D // 4
    row, col = lax.axis_index("row"), lax.axis_index("col")
    z, y = row // 2, row % 2
    x, c = col // 2, col % 2
    ypeer = (row + 1 - 2 * y, col)
    cpeer = (row, col + 1 - 2 * c)
    xpeer = (row, (1 - x) * 2 + c)
    dpeer = (row, (1 - x) * 2 + 1 - c)

    def zdev(zz):
        return (zz * 2 + y, col)

    def rc(src, dst, ss, rs, dev):
        return pltpu.make_async_remote_copy(
            src_ref=src, dst_ref=dst, send_sem=ss, recv_sem=rs, device_id=dev, device_id_type=MESH
        )

    def loop(n, body, first=0):
        def step(i, carry):
            body(i)
            return carry

        lax.fori_loop(first, n, step, 0)

    down0 = PW + 2 * F
    CH = [(0, PW)] + [(PW + 2 * FC * j, 2 * FC) for j in range(3)] + [(down0 + FC * j, FC) for j in range(3)]
    RCH = CH[4:7] + CH[1:4] + [(2 * QW, QW), (0, 2 * QW)]

    own = rows(row, br)
    mine = pl.ds(pl.multiple_of(col * CW, CW), CW)
    local = [
        (wq_h, W.at[own, pl.ds(0, QW)]),
        (wk_h, W.at[own, pl.ds(QW, KW)]),
        (wv_h, W.at[own, pl.ds(QW + KW, KW)]),
        (wot_h, W.at[own, pl.ds(2 * QW, QW)]),
        (tok_h, Tk.at[:, mine]),
        (cot_h, Ct.at[:, mine]),
    ]
    for j in range(3):
        local.append((wg_h.at[:, pl.ds(FC * j, FC)], W.at[own, pl.ds(PW + 2 * FC * j, FC)]))
        local.append((wu_h.at[:, pl.ds(FC * j, FC)], W.at[own, pl.ds(PW + 2 * FC * j + FC, FC)]))
    local.append((wdt_h, W.at[own, pl.ds(down0, F)]))
    local = [pltpu.make_async_copy(s, d, loc_sem.at[i]) for i, (s, d) in enumerate(local)]
    for copy in local:
        copy.start()

    bar = pltpu.get_barrier_semaphore()
    for dev in (ypeer, cpeer, xpeer, dpeer):
        pl.semaphore_signal(bar, inc=1, device_id=dev, device_id_type=MESH)

    def greet(k):
        pl.semaphore_signal(bar, inc=1, device_id=zdev((z + k) % nz), device_id_type=MESH)

    loop(nz, greet, 1)
    pl.semaphore_wait(bar, 4 + nz - 1)

    def wblk(ch, zz, yy):
        start, width = CH[ch]
        return W.at[rows(zz * 2 + yy, br), pl.ds(start, width)]

    def ag_z(ch, k, src):
        b = wblk(ch, src, y)
        return rc(b, b, agz_s.at[ch, k], agz_r.at[ch, k], zdev((z + k) % nz))

    def ag_y(ch, k, src, yy):
        b = wblk(ch, src, yy)
        return rc(b, b, agy_s.at[ch, k], agy_r.at[ch, k], ypeer)

    def ag_own(ch):
        ag_y(ch, 0, z, y).start()
        loop(nz, lambda k: ag_z(ch, k, z).start(), 1)

    def ag_fwd(ch):
        def step(k):
            src = (z + nz - k) % nz
            ag_z(ch, k, src).wait_recv()
            ag_y(ch, k, src, y).start()

        loop(nz, step, 1)

    def ag_wait(ch):
        loop(nz, lambda k: ag_y(ch, k, (z + nz - k) % nz, 1 - y).wait_recv())

    def ag_done(ch):
        loop(nz, lambda k: ag_y(ch, k, (z + nz - k) % nz, y).wait_send())
        loop(nz, lambda k: ag_z(ch, k, z).wait_send(), 1)

    def cag(n, block):
        def copy(i, d, dev):
            return rc(block(d), block(d), cag_s.at[n, i], cag_r.at[n, i], dev)

        def start():
            copy(0, col, cpeer).start()
            copy(1, col, xpeer).start()

        def forward():
            copy(1, (1 - x) * 2 + c, xpeer).wait_recv()
            copy(2, (1 - x) * 2 + c, cpeer).start()

        def wait():
            copy(0, x * 2 + 1 - c, cpeer).wait_recv()
            copy(2, (1 - x) * 2 + 1 - c, cpeer).wait_recv()

        def done():
            copy(0, col, cpeer).wait_send()
            copy(1, col, xpeer).wait_send()
            copy(2, (1 - x) * 2 + c, cpeer).wait_send()

        return start, forward, wait, done

    def col_block(ref):
        return lambda d: ref.at[:, pl.ds(pl.multiple_of(d * CW, CW), CW)]

    def row_block(ref):
        return lambda d: ref.at[rows(d, RB), :]

    tok_start, tok_forward, tok_wait, tok_done = cag(0, col_block(Tk))
    cot_start, cot_forward, cot_wait, cot_done = cag(1, col_block(Ct))
    nf_start, nf_forward, nf_wait, nf_done = cag(2, row_block(NF))
    rl_start, rl_forward, rl_wait, rl_done = cag(3, row_block(Ct))

    def crs(n, A, B, S):
        def to_core(i, xx, cc):
            return rc(PB.at[rows(xx * 2 + cc, RB), :], A(xx), crs_s.at[n, i], crs_r.at[n, i], cpeer)

        def to_x():
            return rc(S, B, crs_s.at[n, 2], crs_r.at[n, 2], xpeer)

        def produce(part):
            def step(i):
                xx = jnp.where(i < 2, 1 - x, x)
                cc = jnp.where(i % 2 == 0, 1 - c, c)
                PB[rows(xx * 2 + cc, RB), :] = part(xx * 2 + cc).astype(bf16)

                @pl.when(i % 2 == 0)
                def _():
                    to_core(i // 2, xx, 1 - c).start()

            loop(4, step)

        def middle():
            to_core(0, 1 - x, c).wait_recv()

            def step(i):
                r = rows(i, 32)
                block = PB[pl.ds(pl.multiple_of(((1 - x) * 2 + c) * RB + i * 32, 32), 32), :]
                S[r, :] = (block.astype(f32) + A(1 - x)[r, :].astype(f32)).astype(bf16)

            loop(RB // 32, step)
            to_x().start()

        def wait():
            to_core(1, x, c).wait_recv()
            to_x().wait_recv()

        def total(i, n):
            r = rows(i, n)
            block = PB[pl.ds(pl.multiple_of(col * RB + i * n, n), n), :].astype(f32)
            return block + A(x)[r, :].astype(f32) + B[r, :].astype(f32)

        def done():
            to_core(0, 1 - x, 1 - c).wait_send()
            to_core(1, x, 1 - c).wait_send()
            to_x().wait_send()

        return produce, middle, wait, total, done

    def gcol(ch):
        start, width = RCH[ch]
        return (G, start - PW, width) if start >= PW else (W, down0 + start, width)

    def gblk(ch, zz, yy):
        ref, start, width = gcol(ch)
        return ref.at[rows(zz * 2 + yy, br), pl.ds(start, width)]

    def rs_y(ch, zz, yy):
        start, width = RCH[ch]
        return rc(
            gblk(ch, zz, yy), RY.at[zz, :, pl.ds(start, width)], rsy_s.at[ch, zz], rsy_r.at[ch, zz], ypeer
        )

    def rs_z(ch, k):
        start, width = RCH[ch]
        part = pl.ds(start, width)
        zz = (z + k) % nz
        return rc(RY.at[zz, :, part], RZ.at[k - 1, :, part], rsz_s.at[ch, k], rsz_r.at[ch, k], zdev(zz))

    zper = RB // (2 * br)

    def grad_step(i):
        return (row * br // RB + 1 + i) % (D // RB)

    def rs_send(ch, dblk):
        loop(zper, lambda s: rs_y(ch, dblk * zper + s, 1 - y).start())

    def rs_mid(ch):
        ref, gstart, width = gcol(ch)
        start = RCH[ch][0]

        def step(k):
            zz = (z + k) % nz
            rs_y(ch, zz, y).wait_recv()

            def add(i):
                r = rows(i, 16)
                g = ref[pl.ds(pl.multiple_of((zz * 2 + y) * br + i * 16, 16), 16), pl.ds(gstart, width)]
                t = RY[zz, r, pl.ds(start, width)]
                RY[zz, r, pl.ds(start, width)] = (g.astype(f32) + t.astype(f32)).astype(bf16)

            loop(br // 16, add)
            rs_z(ch, k).start()

        loop(nz, step, 1)

    def outs(ch):
        start, width = RCH[ch]
        if start >= down0:
            pairs = [(start, width, gdown_h, start - down0)]
        elif start >= PW:
            j = (start - PW) // (2 * FC)
            pairs = [(start, FC, ggate_h, FC * j), (start + FC, FC, gup_h, FC * j)]
        else:
            pairs = [(start, width, gattn_h, start)]
        return [
            pltpu.make_async_copy(GF.at[:, pl.ds(s, w)], ref.at[:, pl.ds(at, w)], out_sem.at[2 * ch + i])
            for i, (s, w, ref, at) in enumerate(pairs)
        ]

    def rs_fin(ch):
        ref, gstart, width = gcol(ch)
        part = pl.ds(RCH[ch][0], width)
        rs_y(ch, z, y).wait_recv()
        loop(nz, lambda k: rs_z(ch, k).wait_recv(), 1)

        def add(i):
            r = rows(i, 16)
            g = ref[pl.ds(pl.multiple_of(row * br + i * 16, 16), 16), pl.ds(gstart, width)]
            total = g.astype(f32) + RY[z, r, part].astype(f32)
            total = lax.fori_loop(0, nz - 1, lambda k, t: t + RZ[k, r, part].astype(f32), total)
            GF[r, part] = total

        loop(br // 16, add)
        for copy in outs(ch):
            copy.start()

    def rs_done(ch):
        loop(nz, lambda zz: rs_y(ch, zz, 1 - y).wait_send())
        loop(nz, lambda k: rs_z(ch, k).wait_send(), 1)
        for copy in outs(ch):
            copy.wait()

    for i in range(4):
        local[i].wait()
    ag_own(0)
    local[4].wait()
    tok_start()

    seg = seg_ref[...]
    first = jnp.zeros((1, T), jnp.int32)
    for d in range(ids):
        count = jnp.sum((seg == d).astype(f32), axis=1, keepdims=True).astype(jnp.int32)
        first = first + jnp.where(seg > d, count, 0)
    place = lax.broadcasted_iota(jnp.int32, (1, T), 1)
    lane = lax.broadcasted_iota(jnp.int32, (1, 128), 1)
    inverse_freq = jnp.exp((lane % 32).astype(f32) * (-2.0 / 64 * math.log(rope_base)))
    CS[...] = jnp.transpose(jnp.broadcast_to((place - first).astype(f32), (128, T)))

    def tables(i):
        angle = CS[rows(i, 128), :] * inverse_freq
        sine = jnp.sin(angle)
        CS[rows(i, 128), :] = jnp.cos(angle)
        SN[rows(i, 128), :] = jnp.where(lane % 64 < 32, -sine, sine)

    loop(T // 128, tables)
    windows = []
    at = 0
    for i in range(nb):
        start = max(0, RB * i - longest)
        width = RB * (i + 1) - start
        windows.append((start, width, at))
        key_place = lax.broadcasted_iota(jnp.int32, (width, RB), 0) + start
        q_place, q_first = place[:, RB * i : RB * (i + 1)], first[:, RB * i : RB * (i + 1)]
        seen = (key_place <= q_place) & (key_place >= q_first)
        BIAS[pl.ds(at, width), :] = jnp.where(seen, 0.0, -1e30).astype(bf16)
        at += width
    half_a = lax.broadcasted_iota(jnp.int32, (128, 128), 0) // 64
    half_b = lax.broadcasted_iota(jnp.int32, (128, 128), 1) // 64
    mean_matrix = jnp.where(half_a == half_b, 1.0 / 64, 0.0).astype(bf16)

    def head_mean(v):
        high = v.astype(bf16)
        low = (v - high.astype(f32)).astype(bf16)
        return dot_nn(high, mean_matrix) + dot_nn(low, mean_matrix)

    def turn(v):
        return jnp.where(lane % 64 < 32, pltpu.roll(v, 96, 1), pltpu.roll(v, 32, 1))

    gain_q = jnp.concatenate([gq_ref[...], gq_ref[...]], axis=1)
    gain_k = jnp.concatenate([gk_ref[...], gk_ref[...]], axis=1)
    ga = ga_ref[...]
    gf = gf_ref[...]

    for i in range(6, 12):
        local[i].wait()
    ag_own(1)
    tok_forward()
    local[5].wait()
    cot_start()
    tok_wait()

    def norm_tokens(i):
        t = Tk[rows(i, 128), :].astype(f32)
        r = lax.rsqrt(jnp.mean(t * t, axis=1, keepdims=True) + epsilon)
        R1[rows(i, 128), :] = jnp.broadcast_to(r, (128, 128))
        Nm[rows(i, 128), :] = (t * r * ga).astype(bf16)

    loop(T // 128, norm_tokens)
    ag_fwd(0)
    local[12].wait()
    ag_own(2)
    ag_wait(0)

    def project(i):
        r = rows(i, RB)
        PRE[r, :] = dot_nn(Nm[r, :], W[:, pl.ds(0, 2 * QW)])
        cos, sin = CS[r, :], SN[r, :]
        for p in range(3):
            v = PRE[r, pl.ds(128 * p, 128)]
            n = v * lax.rsqrt(head_mean(v * v) + epsilon)
            u = n * (gain_q if p < 2 else gain_k)
            u = (u * cos + turn(u) * sin).astype(bf16)
            if p < 2:
                u = u * jnp.asarray(0.125, bf16)
                QS[p, 0, r, :] = u[:, :64]
                QS[p, 1, r, :] = u[:, 64:]
            else:
                KS[0, r, :] = u[:, :64]
                KS[1, r, :] = u[:, 64:]
                ut = jnp.transpose(u)
                KT[0, :, r] = ut[:64, :]
                KT[1, :, r] = ut[64:, :]
        v = PRE[r, pl.ds(384, 128)].astype(bf16)
        VS[0, r, :] = v[:, :64]
        VS[1, r, :] = v[:, 64:]
        vt = jnp.transpose(v)
        VT[0, :, r] = vt[:64, :]
        VT[1, :, r] = vt[64:, :]

    loop(nb, project)

    def attend(i):
        start, width, at = windows[i]
        keys = pl.ds(start, width)
        r = pl.ds(RB * i, RB)

        def step(h):
            q = QS[h, :, r, :].reshape(2 * RB, 64)
            bias = BIAS[pl.ds(at, width), :].astype(f32)
            s = dot_nt(KS[h, keys, :], q) + jnp.concatenate([bias, bias], axis=1)
            e = jnp.exp(s)
            inv = 1.0 / jnp.sum(e, axis=0, keepdims=True)
            INV[h, pl.ds(i, 1), :] = inv
            o = dot_nn(VT[h, :, keys], (e * inv).astype(bf16))
            o = jnp.concatenate([o[:, :RB], o[:, RB:]], axis=0)
            MX[r, pl.ds(pl.multiple_of(h * 128, 128), 128)] = jnp.transpose(o).astype(bf16)

        loop(2, step)

    attend(0)
    attend(1)
    ag_fwd(1)
    ag_own(3)
    cot_forward()
    attend(2)
    attend(3)
    a_produce, a_middle, a_wait, a_total, a_done = crs(0, lambda i: A0.at[i], B0, S0)
    a_produce(lambda d: dot_nt(MX[rows(d, RB), :], W[:, pl.ds(2 * QW, QW)]))
    a_middle()
    ag_fwd(2)
    ag_own(4)
    a_wait()

    def after_attention(i):
        r = rows(i, 32)
        mine_rows = pl.ds(pl.multiple_of(col * RB + i * 32, 32), 32)
        v = Tk[mine_rows, :].astype(f32) + a_total(i, 32)
        RES[r, :] = v
        n = v * lax.rsqrt(jnp.mean(v * v, axis=1, keepdims=True) + epsilon)
        NF[mine_rows, :] = (n * gf).astype(bf16)

    loop(RB // 32, after_attention)
    nf_start()
    a_done()
    cot_wait()
    cot_done()
    ag_own(5)
    ag_own(6)
    nf_forward()
    nf_wait()
    nf_done()

    def ffn(j):
        def step(i):
            r = rows(i, RB)
            n = NF[r, :]
            gate = dot_nn(n, W[:, pl.ds(PW + 2 * FC * j, FC)])
            up = dot_nn(n, W[:, pl.ds(PW + 2 * FC * j + FC, FC)])
            sig = 1.0 / (1.0 + jnp.exp(-gate))
            act = gate * sig
            HID[r, pl.ds(FC * j, FC)] = (act * up).astype(bf16)
            GG[r, pl.ds(2 * FC * j, FC)] = (up * (sig + act * (1.0 - sig))).astype(bf16)
            GG[r, pl.ds(2 * FC * j + FC, FC)] = act.astype(bf16)

        loop(nb, step)

    def weight_grad(left, pieces):
        def step(i):
            d = grad_step(i)
            lt = jnp.transpose(left[:, rows(d, RB)])
            for ch, right in pieces:
                ref, start, width = gcol(ch)
                ref[rows(d, RB), pl.ds(start, width)] = dot_nn(lt, right[...]).astype(bf16)
                rs_send(ch, d)

        loop(D // RB, step)

    for j in range(3):
        ag_wait(1 + j)
        ffn(j)
        if j == 0:
            ag_fwd(3)
        else:
            ag_fwd(3 + j)
        weight_grad(Ct, [(j, HID.at[:, pl.ds(FC * j, FC)])])
        if j > 0:
            rs_mid(j - 1)
    ag_fwd(6)
    for j in range(3):
        ag_wait(4 + j)

        def grad_hidden(i, j=j):
            r = rows(i, RB)
            gh = dot_nn(Ct[r, :], W[:, pl.ds(down0 + FC * j, FC)])
            a, b = pl.ds(2 * FC * j, FC), pl.ds(2 * FC * j + FC, FC)
            GG[r, a] = (gh * GG[r, a].astype(f32)).astype(bf16)
            GG[r, b] = (gh * GG[r, b].astype(f32)).astype(bf16)

        loop(nb, grad_hidden)
    n_produce, n_middle, n_wait, n_total, n_done = crs(1, lambda i: A0.at[i], B0, S0)
    n_produce(lambda d: dot_nt(GG[rows(d, RB), :], W[:, pl.ds(PW, 2 * F)]))
    n_middle()
    rs_mid(2)
    weight_grad(NF, [(3 + j, GG.at[:, pl.ds(2 * FC * j, 2 * FC)]) for j in range(3)])
    n_wait()
    VEC[...] = jnp.zeros(VEC.shape, f32)

    def after_ffn(i):
        r = rows(i, 32)
        mine_rows = pl.ds(pl.multiple_of(col * RB + i * 32, 32), 32)
        gy = n_total(i, 32)
        v = RES[r, :]
        inv = lax.rsqrt(jnp.mean(v * v, axis=1, keepdims=True) + epsilon)
        n = v * inv
        VEC[1:2, :] += jnp.sum(gy * n, axis=0, keepdims=True)
        g = gy * gf
        g = inv * (g - n * jnp.mean(g * n, axis=1, keepdims=True))
        Ct[mine_rows, :] = (Ct[mine_rows, :].astype(f32) + g).astype(bf16)

    loop(RB // 32, after_ffn)
    rl_start()
    n_done()
    rs_mid(3)
    rl_forward()
    rl_wait()

    def grad_mixed(i):
        r = rows(i, RB)
        g = dot_nn(Ct[r, :], W[:, pl.ds(2 * QW, QW)]).astype(bf16)
        for p in range(2):
            DO[p, 0, r, :] = g[:, 128 * p : 128 * p + 64]
            DO[p, 1, r, :] = g[:, 128 * p + 64 : 128 * p + 128]

    loop(nb, grad_mixed)
    b_produce, b_middle, b_wait, b_total, b_done = crs(
        2, lambda i: NF.at[rows(i, RB), :], NF.at[pl.ds(2 * RB, RB), :], NF.at[pl.ds(3 * RB, RB), :]
    )
    b_produce(lambda d: dot_nt(HID[rows(d, RB), :], W[:, pl.ds(down0, F)]))
    b_middle()
    for ch in range(7):
        ag_done(ch)
    weight_grad(Ct, [(6, MX)])
    rs_mid(4)
    DK[...] = jnp.zeros(DK.shape, f32)
    DV[...] = jnp.zeros(DV.shape, f32)

    def attend_back(i):
        start, width, at = windows[i]
        keys = pl.ds(start, width)
        r = pl.ds(RB * i, RB)

        def step(h):
            q = QS[h, :, r, :].reshape(2 * RB, 64)
            do = DO[h, :, r, :].reshape(2 * RB, 64)
            bias = BIAS[pl.ds(at, width), :].astype(f32)
            s = dot_nt(KS[h, keys, :], q) + jnp.concatenate([bias, bias], axis=1)
            p = jnp.exp(s) * INV[h, pl.ds(i, 1), :]
            dp = dot_nt(VS[h, keys, :], do)
            DV[h, keys, :] += dot_nn(p.astype(bf16), do)
            ds = (p * (dp - jnp.sum(p * dp, axis=0, keepdims=True))).astype(bf16)
            DK[h, keys, :] += dot_nn(ds, q)
            g = dot_nn(KT[h, :, keys], ds) * 0.125
            g = jnp.concatenate([g[:, :RB], g[:, RB:]], axis=0)
            DQ[r, pl.ds(pl.multiple_of(h * 128, 128), 128)] = jnp.transpose(g)

        loop(2, step)

    attend_back(0)
    attend_back(1)
    rs_mid(5)
    b_wait()

    def finish(i):
        LO[rows(i, 32), :] = (RES[rows(i, 32), :] + b_total(i, 32)).astype(bf16)

    loop(RB // 32, finish)

    def lo_copy(i, d, dev):
        return rc(
            LO.at[:, pl.ds(pl.multiple_of(d * CW, CW), CW)], LOC.at[rows(col, RB), :], lo_s.at[i], lo_r.at[i], dev
        )

    others = [(0, x * 2 + 1 - c, cpeer), (1, (1 - x) * 2 + c, xpeer), (2, (1 - x) * 2 + 1 - c, dpeer)]
    for i, d, dev in others:
        lo_copy(i, d, dev).start()
    LOC[rows(col, RB), :] = LO[:, mine]
    attend_back(2)
    rs_mid(6)
    attend_back(3)

    def project_back(i):
        r = rows(i, RB)
        cos, sin = CS[r, :], SN[r, :]
        for p in range(3):
            g = DQ[r, pl.ds(128 * p, 128)] if p < 2 else jnp.concatenate([DK[0, r, :], DK[1, r, :]], axis=1)
            g = g * cos - turn(g) * sin
            v = PRE[r, pl.ds(128 * p, 128)]
            inv = lax.rsqrt(head_mean(v * v) + epsilon)
            n = v * inv
            s = pl.ds(0 if p < 2 else 128, 128)
            VEC[2:3, s] += jnp.sum(g * n, axis=0, keepdims=True)
            g = g * (gain_q if p < 2 else gain_k)
            HID[r, pl.ds(128 * p, 128)] = (inv * (g - n * head_mean(g * n))).astype(bf16)
        HID[r, pl.ds(384, 128)] = jnp.concatenate([DV[0, r, :], DV[1, r, :]], axis=1).astype(bf16)

    loop(nb, project_back)
    weight_grad(Nm, [(7, HID.at[:, pl.ds(0, 2 * QW)])])

    def gn_core(i, k, xx, cc):
        d = xx * 2 + cc
        return rc(
            PB.at[rows(i, RB), pl.ds(pl.multiple_of(d * CW, CW), CW)],
            AC.at[rows(i, RB), pl.ds(pl.multiple_of(xx * CW, CW), CW)],
            gn_s.at[i, k], gn_r.at[i, k], cpeer,
        )

    def gn_x(i):
        return rc(SC.at[rows(i, RB), :], BC.at[rows(i, RB), :], gn_s.at[i, 2], gn_r.at[i, 2], xpeer)

    b_done()

    def gn_produce(i):
        r = rows(i, RB)
        g = dot_nt(HID[r, pl.ds(0, 2 * QW)], W[:, pl.ds(0, 2 * QW)])
        PB[r, :] = g.astype(bf16)
        gn_core(i, 0, 1 - x, 1 - c).start()
        gn_core(i, 1, x, 1 - c).start()
        g = g * (Tk[r, :].astype(f32) * R1[r, pl.ds(0, 1)])
        VEC[0:1, :] += jnp.sum(g, axis=0, keepdims=True)
        s = jnp.sum(g * ga, axis=1, keepdims=True)
        VEC[3:4, r] = jnp.transpose(jnp.broadcast_to(s, (RB, 128)))[0:1, :]

    loop(nb, gn_produce)

    def vec_copy(i, src, dst, dev):
        return rc(src, dst, vec_s.at[i], vec_r.at[i], dev)

    vec_c = vec_copy(0, VEC, VC, cpeer)
    vec_c.start()

    def gn_middle(i):
        r = rows(i, RB)
        gn_core(i, 0, 1 - x, c).wait_recv()
        a = PB[r, pl.ds(pl.multiple_of(((1 - x) * 2 + c) * CW, CW), CW)].astype(f32)
        b = AC[r, pl.ds(pl.multiple_of((1 - x) * CW, CW), CW)].astype(f32)
        SC[r, :] = (a + b).astype(bf16)
        gn_x(i).start()

    loop(nb, gn_middle)
    vec_c.wait_recv()
    vec_c.wait_send()
    VEC[...] += VC[...]
    vec_x = vec_copy(1, VEC, VX, xpeer)
    vec_x.start()
    rs_fin(0)
    rs_fin(1)
    rs_fin(2)
    rs_mid(7)
    vec_x.wait_recv()
    vec_x.wait_send()
    VEC[...] += VX[...]
    vec_y = vec_copy(2, VEC, VY, ypeer)
    vec_y.start()

    def gn_finish(i):
        r = rows(i, RB)
        gn_core(i, 1, x, c).wait_recv()
        gn_x(i).wait_recv()
        g = PB[r, mine].astype(f32) + AC[r, pl.ds(pl.multiple_of(x * CW, CW), CW)].astype(f32) + BC[r, :].astype(f32)
        g = g * ga_ref[:, mine]
        inv = R1[r, pl.ds(0, 1)]
        s = jnp.transpose(jnp.broadcast_to(VEC[3:4, r], (128, RB)))[:, 0:1] * (1.0 / D)
        n = Tk[r, mine].astype(f32) * inv
        DQ[r, :] = Ct[r, mine].astype(f32) + inv * (g - n * s)

    loop(nb, gn_finish)
    gt_copy = pltpu.make_async_copy(DQ, gt_h, out_sem.at[16])
    gt_copy.start()
    vec_y.wait_recv()
    vec_y.wait_send()
    VZ[z] = VEC[...] + VY[...]

    def vz_copy(k, src):
        return rc(VZ.at[src], VZ.at[src], vz_s.at[k], vz_r.at[k], zdev((z + k) % nz))

    loop(nz, lambda k: vz_copy(k, z).start(), 1)
    for i, d, dev in others:
        lo_copy(i, d, dev).wait_recv()
    lo_out = pltpu.make_async_copy(LOC, lo_h, out_sem.at[17])
    lo_out.start()
    for ch in range(3, 8):
        rs_fin(ch)
    loop(nz, lambda k: vz_copy(k, (z + nz - k) % nz).wait_recv(), 1)
    gain_ref[...] = lax.fori_loop(1, nz, lambda k, t: t + VZ[k], VZ[0])

    tok_done()
    rl_done()
    for i, d, dev in others:
        lo_copy(i, d, dev).wait_send()

    def gn_done(i):
        gn_core(i, 0, 1 - x, 1 - c).wait_send()
        gn_core(i, 1, x, 1 - c).wait_send()
        gn_x(i).wait_send()

    loop(nb, gn_done)
    loop(nz, lambda k: vz_copy(k, z).wait_send(), 1)
    for ch in range(8):
        rs_done(ch)
    gt_copy.wait()
    lo_out.wait()


def per_device(
    n_row, tokens, segment_ids, w_query, key_matrix, value_matrix, w_out, w_gate, w_up, w_down,
    norm_attn, norm_ffn, norm_query, norm_key, cotangent,
):
    T, CW = tokens.shape
    br, QW = w_query.shape
    KW = key_matrix.shape[1]
    F = w_gate.shape[1]
    D = br * n_row
    nz = n_row // 2
    PW = 2 * QW + 2 * KW
    WW = PW + 3 * F
    nb = T // RB
    area = sum(RB * (i + 1) - max(0, RB * i - longest) for i in range(nb))
    vm, sem = pltpu.VMEM, pltpu.SemaphoreType.DMA
    scratch = [
        vm((D, WW), bf16), vm((D, 3 * F), bf16), vm((nz, br, WW), bf16), vm((nz - 1, br, WW), bf16),
        vm((br, WW), f32), vm((T, D), bf16), vm((T, D), bf16), vm((T, D), bf16), vm((T, 128), f32),
        vm((T, 2 * QW), f32), vm((2, 2, T, 64), bf16), vm((2, T, 64), bf16), vm((2, T, 64), bf16),
        vm((2, 64, T), bf16), vm((2, 64, T), bf16), vm((2, 2, T, 64), bf16), vm((T, QW), bf16),
        vm((T, D), bf16), vm((2, RB, D), bf16), vm((RB, D), bf16), vm((RB, D), bf16), vm((RB, D), f32),
        vm((T, D), bf16), vm((T, 2 * F), bf16), vm((T, F), bf16),
        vm((T, 128), f32), vm((T, 128), f32), vm((area, RB), bf16), vm((2, 8, 2 * RB), f32),
        vm((T, QW), f32), vm((2, T, 64), f32), vm((2, T, 64), f32),
        vm((T, 2 * CW), bf16), vm((T, CW), bf16), vm((T, CW), bf16), vm((RB, D), bf16), vm((T, CW), bf16),
        vm((8, D), f32), vm((8, D), f32), vm((8, D), f32), vm((8, D), f32), vm((nz, 8, D), f32),
        sem((13,)), sem((7, nz)), sem((7, nz)), sem((7, nz)), sem((7, nz)),
        sem((8, nz)), sem((8, nz)), sem((8, nz)), sem((8, nz)),
        sem((4, 3)), sem((4, 3)), sem((3, 3)), sem((3, 3)), sem((nb, 3)), sem((nb, 3)), sem((3,)), sem((3,)),
        sem((3,)), sem((3,)), sem((nz,)), sem((nz,)), sem((18,)),
    ]
    whole, hbm = pl.BlockSpec(memory_space=pltpu.VMEM), pl.BlockSpec(memory_space=pl.ANY)
    shape = jax.ShapeDtypeStruct
    outs = pl.pallas_call(
        functools.partial(layer_kernel, nz),
        out_shape=(
            shape((T, CW), bf16), shape((T, CW), f32), shape((br, PW), f32), shape((br, F), f32),
            shape((br, F), f32), shape((br, F), f32), shape((8, D), f32),
        ),
        in_specs=[hbm, whole] + [hbm] * 7 + [whole] * 4 + [hbm],
        out_specs=(hbm,) * 6 + (whole,),
        scratch_shapes=scratch,
        compiler_params=pltpu.CompilerParams(
            collective_id=0, has_side_effects=True, vmem_limit_bytes=64 * 2**20
        ),
        name="layer",
    )(
        tokens, segment_ids, w_query, key_matrix, value_matrix, w_out.T, w_gate, w_up, w_down.T,
        norm_attn[None], norm_ffn[None], norm_query[None], norm_key[None], cotangent,
    )
    layer_out, grad_tokens, g_attn, g_gate, g_up, g_down, gains = outs
    return (
        layer_out, grad_tokens, g_attn[:, :QW], g_attn[:, QW : QW + KW], g_attn[:, QW + KW : 2 * QW],
        g_attn[:, 2 * QW :].T, g_gate, g_up, g_down.T, gains[0], gains[1],
        gains[2, :64] + gains[2, 64:128], gains[2, 128:192] + gains[2, 192:256],
    )


def solution(mesh):
    in_specs = (
        P("row", "col"), P("row", None), P("row", "col"), P("row", "col"), P("row", "col"), P("col", "row"),
        P("row", "col"), P("row", "col"), P("col", "row"), P(), P(), P(), P(), P("row", "col"),
    )
    out_specs = (
        P("row", "col"), P("row", "col"), P("row", "col"), P("row", "col"), P("row", "col"), P("col", "row"),
        P("row", "col"), P("row", "col"), P("col", "row"), P(), P(), P(), P(),
    )
    return jax.shard_map(
        functools.partial(per_device, mesh.shape["row"]),
        mesh=mesh, in_specs=in_specs, out_specs=out_specs, check_vma=False,
    )
```

time: 1170 us -> 269 us (0.23)
  waiting for transfers between devices: 800 us -> 0 us
  Pallas kernels: 0 us -> 250 us
  blocking collectives: 170 us -> 0 us
  matrix products: 102 us -> 0 us
  other arithmetic: 42.6 us -> 1.35 us
  between operations: 17 us -> 0.67 us
    reduce_scatter x8 -> x0, waiting for transfers between devices: 514 us -> none  [the longest x1 99.6 us: per_device(): lax.psum_scatter(grad_down_w, 'row', scatter_dimension=1, tiled=True)]
    pallas_call x0 -> x1, Pallas kernels: none -> 250 us  [per_device(): pl.pallas_call(functools.partial(layer_kernel, nz), out_shape=(shape((T,...]
    psum x3 -> x0, waiting for transfers between devices: 205 us -> none  [the longest x1 82 us: per_device(): attended = lax.psum(attn_partial, 'col')]
    all_gather x4 -> x0, blocking collectives: 130 us -> none  [the longest x1 34.8 us: per_device(): lax.all_gather(key_matrix, 'row', axis=0, tiled=True)]
    dot_general x31 -> x0, matrix products: 88.8 us -> none  [the longest x7 27.6 us: lead_dot(): lax.dot_general(left_mat, right_mat, (((0,), (0,)), ((), ())), preferred_...]
    all_gather x5 -> x0, waiting for transfers between devices: 78.4 us -> none  [the longest x1 56 us: per_device(): lax.all_gather(w_down, 'row', axis=1, tiled=True)]
    psum x1 -> x0, blocking collectives: 39.8 us -> none  [per_device(): lax.psum((attn_gain_term, ffn_gain_term, grad_gain_query, grad_gain_key),...]
    reduce_sum x6 -> x0, other arithmetic: 16.9 us -> none  [the longest x2 10.7 us: gain_norm(): return root_norm(operand) * gain]
  transfers between devices with their start and end apart: 16 -> 0, of which waited for: 13 -> 0; matrix products, arithmetic and copies ran while one was open for 9% -> 0% of each run, Pallas kernels for 0% -> 0%
where the time goes in v1:
time: 269 us; the launch traced here: 266 us
  Pallas kernels  250 us (93%)
  local copies, waits for them, and re-layouts  14.2 us (5%)
    pallas_call x1, Pallas kernels, per_device(): pl.pallas_call(functools.partial(layer_kernel, nz), out_shape=(shape((T,...  250 us
    unnamed x18, local copies, waits for them, and re-layouts  9.56 us

profile of v1, /device:TPU:0, one launch (start us, length us, event | category | flops | bytes accessed | tf_op | source)
XLA Modules:
  0.0 266.4 jit_solution(5573809383060450510)
XLA Ops:
  0.6 1.6 copy.27
  2.2 1.8 copy.28
  4.1 250.2 %layer.1 = (bf16[1024,256]{1,0:T(8,128)(2,1)}, f32[1024,256]{1,0:T(8,128)}, f32[128,768]{1,0:T(8,128)}, f32[128,1152]{1,0:T(8,128)}, f32[128,1152]{1,0:T(8,128)}...) custom-call(bf16[1024,256]{1,0:T(8,128)(2,1)} %tok_h.1, s32[1,1024]{1,0:T(1,128)} %seg_ref.1, bf16[128,256]{1,0:T(8,128)(2,1)} %wq_h.1, ...), custom_call_target="tpu_custom_call" | custom-call | tf_op jit(solution)/shard_map/layer/pallas_call | solution.py:743
  254.2 0.0 copy-start.3
  254.3 1.4 add_bitcast_fusion
  255.6 1.4 fusion.1
  257.0 1.5 fusion
  258.6 1.6 slice_bitcast_fusion
  260.2 0.0 copy-start.4
  260.2 0.8 copy.29
  261.0 0.0 copy-done.3
  261.0 0.0 copy-start
  261.0 1.0 copy.30
  262.0 0.0 copy-done.4
  262.0 0.8 copy.35
  262.8 0.0 copy-done
  262.8 0.0 copy-start.2
  262.8 1.0 copy.36
  263.8 0.5 copy-done.2
  264.3 0.0 copy-start.1
  264.3 0.8 copy.37
  265.1 0.5 copy-done.1
  265.5 0.8 copy.38
Async XLA Ops:
  254.2 6.7 %copy-start.3 = (f32[128,1152]{1,0:T(8,128)S(1)}, f32[128,1152]{1,0:T(8,128)}, u32[]{:S(2)}) copy-start(f32[128,1152]{1,0:T(8,128)} %get-tuple-element.25) | copy-start | bytes 1769476
  260.2 1.8 copy-start.4
  261.0 1.9 copy-start
  262.8 1.4 copy-start.2
  264.3 1.3 copy-start.1

commit v2 on v1

--- a/solution.py
+++ b/solution.py
@@ -31,10 +31,10 @@
 
 def layer_kernel(
     nz,
-    tok_h, seg_ref, wq_h, wk_h, wv_h, wot_h, wg_h, wu_h, wdt_h, ga_ref, gf_ref, gq_ref, gk_ref, cot_h,
-    lo_h, gt_h, gattn_h, ggate_h, gup_h, gdown_h, gain_ref,
-    W, G, RY, RZ, GF, Tk, Ct, Nm, R1, PRE, QS, KS, VS, KT, VT, DO, MX, PB, A0, B0, S0, RES, NF, GG, HID,
-    CS, SN, BIAS, INV, DQ, DK, DV, AC, BC, SC, LO, LOC, VEC, VC, VX, VY, VZ,
+    tok_h, seg_ref, wq_h, wk_h, wv_h, wo_h, wg_h, wu_h, wd_h, ga_ref, gf_ref, gq_ref, gk_ref, cot_h,
+    lo_h, gt_h, gquery_h, gkey_h, gvalue_h, gout_h, ggate_h, gup_h, gdown_h, gain_ref,
+    W, WO, WD, GFO, GFD, G, RY, RZ, GF, Tk, Ct, Nm, R1, PRE, QS, KS, VS, KT, VT, DO, MX, PB, A0, B0, S0, RES, NF, GG, HID,
+    CS, SN, BIAS, INV, DQ, DK, DV, AC, BC, SC, LOC, VEC, VC, VX, VY, VZ,
     loc_sem, agz_s, agz_r, agy_s, agy_r, rsy_s, rsy_r, rsz_s, rsz_r,
     cag_s, cag_r, crs_s, crs_r, gn_s, gn_r, lo_s, lo_r, vec_s, vec_r, vz_s, vz_r, out_sem,
 ):
@@ -53,9 +53,23 @@
     cpeer = (row, col + 1 - 2 * c)
     xpeer = (row, (1 - x) * 2 + c)
     dpeer = (row, (1 - x) * 2 + 1 - c)
+    tree = nz == 4
+    partner = z + 1 - 2 * (z % 2)
+    is_middle = (z == 1) | (z == 2)
+    near, far = 2 - z // 2, 3 - 3 * (z // 2)
 
     def zdev(zz):
         return (zz * 2 + y, col)
+
+    def zsrc(k):
+        if tree:
+            return jnp.where(k == 0, z, jnp.where(k == 1, partner, jnp.where(k == 2, near, far)))
+        return (z + nz - k) % nz
+
+    def zorder(i):
+        if tree:
+            return zsrc(jnp.where(i == 3, 0, jnp.where(i == 2, 1, i + 2)))
+        return (z + 1 + i) % nz
 
     def rc(src, dst, ss, rs, dev):
         return pltpu.make_async_remote_copy(
@@ -79,14 +93,14 @@
         (wq_h, W.at[own, pl.ds(0, QW)]),
         (wk_h, W.at[own, pl.ds(QW, KW)]),
         (wv_h, W.at[own, pl.ds(QW + KW, KW)]),
-        (wot_h, W.at[own, pl.ds(2 * QW, QW)]),
+        (wo_h, WO),
         (tok_h, Tk.at[:, mine]),
         (cot_h, Ct.at[:, mine]),
     ]
     for j in range(3):
         local.append((wg_h.at[:, pl.ds(FC * j, FC)], W.at[own, pl.ds(PW + 2 * FC * j, FC)]))
         local.append((wu_h.at[:, pl.ds(FC * j, FC)], W.at[own, pl.ds(PW + 2 * FC * j + FC, FC)]))
-    local.append((wdt_h, W.at[own, pl.ds(down0, F)]))
+    local.append((wd_h, WD))
     local = [pltpu.make_async_copy(s, d, loc_sem.at[i]) for i, (s, d) in enumerate(local)]
     for copy in local:
         copy.start()
@@ -105,9 +119,9 @@
         start, width = CH[ch]
         return W.at[rows(zz * 2 + yy, br), pl.ds(start, width)]
 
-    def ag_z(ch, k, src):
+    def ag_z(ch, k, src, slot, dev):
         b = wblk(ch, src, y)
-        return rc(b, b, agz_s.at[ch, k], agz_r.at[ch, k], zdev((z + k) % nz))
+        return rc(b, b, agz_s.at[ch, k], agz_r.at[ch, slot], zdev(dev))
 
     def ag_y(ch, k, src, yy):
         b = wblk(ch, src, yy)
@@ -115,22 +129,45 @@
 
     def ag_own(ch):
         ag_y(ch, 0, z, y).start()
-        loop(nz, lambda k: ag_z(ch, k, z).start(), 1)
-
-    def ag_fwd(ch):
+        if tree:
+            ag_z(ch, 0, z, 1, partner).start()
+            ag_z(ch, 1, z, jnp.where(is_middle, 2, 3), near).start()
+        else:
+            loop(nz, lambda k: ag_z(ch, k, z, k, (z + k) % nz).start(), 1)
+
+    def ag_fwd(ch, only=None):
         def step(k):
-            src = (z + nz - k) % nz
-            ag_z(ch, k, src).wait_recv()
+            src = zsrc(k)
+            ag_z(ch, k, src, k, partner).wait_recv()
+            if tree:
+
+                @pl.when((k >= 2) & is_middle)
+                def _():
+                    ag_z(ch, k, src, k, partner).start()
+
             ag_y(ch, k, src, y).start()
 
-        loop(nz, step, 1)
+        if only is None:
+            loop(nz, step, 1)
+        else:
+            loop(only[1], step, only[0])
 
     def ag_wait(ch):
-        loop(nz, lambda k: ag_y(ch, k, (z + nz - k) % nz, 1 - y).wait_recv())
+        loop(nz, lambda k: ag_y(ch, k, zsrc(k), 1 - y).wait_recv())
 
     def ag_done(ch):
-        loop(nz, lambda k: ag_y(ch, k, (z + nz - k) % nz, y).wait_send())
-        loop(nz, lambda k: ag_z(ch, k, z).wait_send(), 1)
+        loop(nz, lambda k: ag_y(ch, k, zsrc(k), y).wait_send())
+        if tree:
+            ag_z(ch, 0, z, 1, partner).wait_send()
+            ag_z(ch, 1, z, 2, near).wait_send()
+
+            @pl.when(is_middle)
+            def _():
+                ag_z(ch, 2, near, 2, partner).wait_send()
+                ag_z(ch, 3, far, 3, partner).wait_send()
+
+        else:
+            loop(nz, lambda k: ag_z(ch, k, z, k, z).wait_send(), 1)
 
     def cag(n, block):
         def copy(i, d, dev):
@@ -226,81 +263,133 @@
             gblk(ch, zz, yy), RY.at[zz, :, pl.ds(start, width)], rsy_s.at[ch, zz], rsy_r.at[ch, zz], ypeer
         )
 
-    def rs_z(ch, k):
-        start, width = RCH[ch]
-        part = pl.ds(start, width)
-        zz = (z + k) % nz
-        return rc(RY.at[zz, :, part], RZ.at[k - 1, :, part], rsz_s.at[ch, k], rsz_r.at[ch, k], zdev(zz))
+    def rs_z(ch, k, zz, slot, dev):
+        part = pl.ds(RCH[ch][0], RCH[ch][1])
+        return rc(RY.at[zz, :, part], RZ.at[slot, :, part], rsz_s.at[ch, k], rsz_r.at[ch, slot], zdev(dev))
 
     zper = RB // (2 * br)
 
     def grad_step(i):
-        return (row * br // RB + 1 + i) % (D // RB)
+        return zorder(i) if tree else (row * br // RB + 1 + i) % (D // RB)
 
     def rs_send(ch, dblk):
         loop(zper, lambda s: rs_y(ch, dblk * zper + s, 1 - y).start())
 
+    def rs_add(ch, zz, what):
+        start, width = RCH[ch]
+
+        def add(i):
+            r = rows(i, 16)
+            t = RY[zz, r, pl.ds(start, width)].astype(f32)
+            RY[zz, r, pl.ds(start, width)] = (what(i).astype(f32) + t).astype(bf16)
+
+        loop(br // 16, add)
+
     def rs_mid(ch):
         ref, gstart, width = gcol(ch)
-        start = RCH[ch][0]
-
-        def step(k):
-            zz = (z + k) % nz
+
+        def step(i):
+            zz = zorder(i)
             rs_y(ch, zz, y).wait_recv()
-
-            def add(i):
-                r = rows(i, 16)
-                g = ref[pl.ds(pl.multiple_of((zz * 2 + y) * br + i * 16, 16), 16), pl.ds(gstart, width)]
-                t = RY[zz, r, pl.ds(start, width)]
-                RY[zz, r, pl.ds(start, width)] = (g.astype(f32) + t.astype(f32)).astype(bf16)
-
-            loop(br // 16, add)
-            rs_z(ch, k).start()
-
-        loop(nz, step, 1)
+            rs_add(
+                ch, zz,
+                lambda j: ref[pl.ds(pl.multiple_of((zz * 2 + y) * br + j * 16, 16), 16), pl.ds(gstart, width)],
+            )
+            if tree:
+
+                @pl.when((i == 2) | jnp.logical_not(is_middle))
+                def _():
+                    rs_z(ch, i, zz, i, partner).start()
+
+            else:
+                rs_z(ch, i, zz, i, zz).start()
+
+        loop(nz - 1, step)
+
+    def rs_relay(ch):
+        if tree:
+
+            @pl.when(is_middle)
+            def _():
+                def step(i):
+                    zz = zorder(i)
+                    rs_z(ch, i, zz, i, partner).wait_recv()
+                    rs_add(ch, zz, lambda j: RZ[i, rows(j, 16), pl.ds(RCH[ch][0], RCH[ch][1])])
+                    rs_z(ch, i, zz, 3, zz).start()
+
+                loop(2, step)
 
     def outs(ch):
         start, width = RCH[ch]
         if start >= down0:
-            pairs = [(start, width, gdown_h, start - down0)]
+            pairs = [(GFD.at[pl.ds(start - down0, width), :], gdown_h.at[pl.ds(start - down0, width), :])]
         elif start >= PW:
-            j = (start - PW) // (2 * FC)
-            pairs = [(start, FC, ggate_h, FC * j), (start + FC, FC, gup_h, FC * j)]
+            at = pl.ds((start - PW) // 2, FC)
+            pairs = [
+                (GF.at[:, pl.ds(start - 2 * KW, FC)], ggate_h.at[:, at]),
+                (GF.at[:, pl.ds(start - 2 * KW + FC, FC)], gup_h.at[:, at]),
+            ]
+        elif start == 2 * QW:
+            pairs = [(GFO, gout_h)]
         else:
-            pairs = [(start, width, gattn_h, start)]
-        return [
-            pltpu.make_async_copy(GF.at[:, pl.ds(s, w)], ref.at[:, pl.ds(at, w)], out_sem.at[2 * ch + i])
-            for i, (s, w, ref, at) in enumerate(pairs)
-        ]
+            pairs = [
+                (GF.at[:, pl.ds(0, QW)], gquery_h),
+                (GF.at[:, pl.ds(QW, KW)], gkey_h),
+                (GF.at[:, pl.ds(QW + KW, KW)], gvalue_h),
+            ]
+        return [pltpu.make_async_copy(a, b, out_sem.at[3 * ch + i]) for i, (a, b) in enumerate(pairs)]
 
     def rs_fin(ch):
         ref, gstart, width = gcol(ch)
-        part = pl.ds(RCH[ch][0], width)
+        start = RCH[ch][0]
         rs_y(ch, z, y).wait_recv()
-        loop(nz, lambda k: rs_z(ch, k).wait_recv(), 1)
-
-        def add(i):
-            r = rows(i, 16)
-            g = ref[pl.ds(pl.multiple_of(row * br + i * 16, 16), 16), pl.ds(gstart, width)]
-            total = g.astype(f32) + RY[z, r, part].astype(f32)
-            total = lax.fori_loop(0, nz - 1, lambda k, t: t + RZ[k, r, part].astype(f32), total)
-            GF[r, part] = total
-
-        loop(br // 16, add)
+        slots = (2, 3) if tree else (0, nz - 2)
+        loop(slots[1] + 1, lambda k: rs_z(ch, 0, z, k, z).wait_recv(), slots[0])
+
+        def total(r0, rn, c0, cn):
+            r = pl.ds(r0, rn)
+            g = ref[pl.ds(pl.multiple_of(row * br + r0, 16), rn), pl.ds(gstart + c0, cn)]
+            part = pl.ds(start + c0, cn)
+            t = g.astype(f32) + RY[z, r, part].astype(f32)
+            return lax.fori_loop(slots[0], slots[1] + 1, lambda k, t: t + RZ[k, r, part].astype(f32), t)
+
+        if start >= down0 or start == 2 * QW:
+            for c0 in range(0, width, 128):
+                t = jnp.transpose(total(0, br, c0, 128))
+                if start >= down0:
+                    GFD[pl.ds(start - down0 + c0, 128), :] = t
+                else:
+                    GFO[pl.ds(c0, 128), :] = t
+        else:
+            at = start - 2 * KW if start >= PW else start
+
+            def add(i):
+                r0 = pl.multiple_of(i * 16, 16)
+                GF[pl.ds(r0, 16), pl.ds(at, width)] = total(r0, 16, 0, width)
+
+            loop(br // 16, add)
         for copy in outs(ch):
             copy.start()
 
     def rs_done(ch):
         loop(nz, lambda zz: rs_y(ch, zz, 1 - y).wait_send())
-        loop(nz, lambda k: rs_z(ch, k).wait_send(), 1)
+        loop(nz - 1, lambda k: rs_z(ch, k, z, 0, z).wait_send())
         for copy in outs(ch):
             copy.wait()
 
     for i in range(4):
         local[i].wait()
+    W[own, pl.ds(2 * QW, QW)] = jnp.transpose(WO[...])
     ag_own(0)
     local[4].wait()
     tok_start()
+    for i in range(6, 12):
+        local[i].wait()
+    ag_own(1)
+    local[12].wait()
+    W[own, pl.ds(down0, F)] = jnp.transpose(WD[...])
+    local[5].wait()
+    cot_start()
 
     seg = seg_ref[...]
     first = jnp.zeros((1, T), jnp.int32)
@@ -347,12 +436,14 @@
     ga = ga_ref[...]
     gf = gf_ref[...]
 
-    for i in range(6, 12):
-        local[i].wait()
-    ag_own(1)
+    ag_fwd(0, (1, 3))
+    if tree:
+
+        @pl.when(is_middle)
+        def _():
+            ag_fwd(0, (3, 4))
+
     tok_forward()
-    local[5].wait()
-    cot_start()
     tok_wait()
 
     def norm_tokens(i):
@@ -362,8 +453,14 @@
         Nm[rows(i, 128), :] = (t * r * ga).astype(bf16)
 
     loop(T // 128, norm_tokens)
-    ag_fwd(0)
-    local[12].wait()
+    if tree:
+
+        @pl.when(jnp.logical_not(is_middle))
+        def _():
+            ag_fwd(0, (3, 4))
+
+    else:
+        ag_fwd(0, (3, nz))
     ag_own(2)
     ag_wait(0)
 
@@ -413,10 +510,10 @@
 
         loop(2, step)
 
+    ag_fwd(1)
+    ag_own(3)
     attend(0)
     attend(1)
-    ag_fwd(1)
-    ag_own(3)
     cot_forward()
     attend(2)
     attend(3)
@@ -440,8 +537,8 @@
     a_done()
     cot_wait()
     cot_done()
+    ag_fwd(3)
     ag_own(5)
-    ag_own(6)
     nf_forward()
     nf_wait()
     nf_done()
@@ -474,14 +571,14 @@
     for j in range(3):
         ag_wait(1 + j)
         ffn(j)
+        ag_fwd(4 + j)
         if j == 0:
-            ag_fwd(3)
-        else:
-            ag_fwd(3 + j)
+            ag_own(6)
         weight_grad(Ct, [(j, HID.at[:, pl.ds(FC * j, FC)])])
         if j > 0:
             rs_mid(j - 1)
-    ag_fwd(6)
+        if j > 1:
+            rs_relay(j - 2)
     for j in range(3):
         ag_wait(4 + j)
 
@@ -496,8 +593,10 @@
     n_produce, n_middle, n_wait, n_total, n_done = crs(1, lambda i: A0.at[i], B0, S0)
     n_produce(lambda d: dot_nt(GG[rows(d, RB), :], W[:, pl.ds(PW, 2 * F)]))
     n_middle()
+    rs_relay(1)
     rs_mid(2)
     weight_grad(NF, [(3 + j, GG.at[:, pl.ds(2 * FC * j, 2 * FC)]) for j in range(3)])
+    rs_relay(2)
     n_wait()
     VEC[...] = jnp.zeros(VEC.shape, f32)
 
@@ -537,6 +636,7 @@
         ag_done(ch)
     weight_grad(Ct, [(6, MX)])
     rs_mid(4)
+    rs_relay(3)
     DK[...] = jnp.zeros(DK.shape, f32)
     DV[...] = jnp.zeros(DV.shape, f32)
 
@@ -564,7 +664,9 @@
     attend_back(0)
     attend_back(1)
     rs_mid(5)
+    rs_relay(4)
     b_wait()
+    LO = S0
 
     def finish(i):
         LO[rows(i, 32), :] = (RES[rows(i, 32), :] + b_total(i, 32)).astype(bf16)
@@ -581,8 +683,10 @@
         lo_copy(i, d, dev).start()
     LOC[rows(col, RB), :] = LO[:, mine]
     attend_back(2)
+    rs_relay(5)
     rs_mid(6)
     attend_back(3)
+    rs_relay(6)
 
     def project_back(i):
         r = rows(i, RB)
@@ -652,6 +756,7 @@
     rs_fin(1)
     rs_fin(2)
     rs_mid(7)
+    rs_relay(7)
     vec_x.wait_recv()
     vec_x.wait_send()
     VEC[...] += VX[...]
@@ -670,7 +775,7 @@
         DQ[r, :] = Ct[r, mine].astype(f32) + inv * (g - n * s)
 
     loop(nb, gn_finish)
-    gt_copy = pltpu.make_async_copy(DQ, gt_h, out_sem.at[16])
+    gt_copy = pltpu.make_async_copy(DQ, gt_h, out_sem.at[24])
     gt_copy.start()
     vec_y.wait_recv()
     vec_y.wait_send()
@@ -682,7 +787,7 @@
     loop(nz, lambda k: vz_copy(k, z).start(), 1)
     for i, d, dev in others:
         lo_copy(i, d, dev).wait_recv()
-    lo_out = pltpu.make_async_copy(LOC, lo_h, out_sem.at[17])
+    lo_out = pltpu.make_async_copy(LOC, lo_h, out_sem.at[25])
     lo_out.start()
     for ch in range(3, 8):
         rs_fin(ch)
@@ -705,6 +810,24 @@
         rs_done(ch)
     gt_copy.wait()
     lo_out.wait()
+
+
+def hand_out(*refs):
+    sources, gains, targets, held, sem = refs[:9], refs[9], refs[10:19], refs[23:32], refs[32]
+    loads = [pltpu.make_async_copy(a, b, sem.at[0, i]) for i, (a, b) in enumerate(zip(sources, held))]
+    stores = [pltpu.make_async_copy(a, b, sem.at[1, i]) for i, (a, b) in enumerate(zip(held, targets))]
+    for copy in loads:
+        copy.start()
+    attn, ffn, query, key = refs[19:23]
+    attn[...] = gains[0:1, :]
+    ffn[...] = gains[1:2, :]
+    query[...] = gains[2:3, 0:64] + gains[2:3, 64:128]
+    key[...] = gains[2:3, 128:192] + gains[2:3, 192:256]
+    for load, store in zip(loads, stores):
+        load.wait()
+        store.start()
+    for store in stores:
+        store.wait()
 
 
 def per_device(
@@ -723,46 +846,54 @@
     area = sum(RB * (i + 1) - max(0, RB * i - longest) for i in range(nb))
     vm, sem = pltpu.VMEM, pltpu.SemaphoreType.DMA
     scratch = [
-        vm((D, WW), bf16), vm((D, 3 * F), bf16), vm((nz, br, WW), bf16), vm((nz - 1, br, WW), bf16),
-        vm((br, WW), f32), vm((T, D), bf16), vm((T, D), bf16), vm((T, D), bf16), vm((T, 128), f32),
+        vm((D, WW), bf16), vm((QW, br), bf16), vm((F, br), bf16), vm((QW, br), f32), vm((F, br), f32),
+        vm((D, 3 * F), bf16), vm((nz, br, WW), bf16), vm((4 if nz == 4 else nz - 1, br, WW), bf16),
+        vm((br, 2 * QW + 2 * F), f32), vm((T, D), bf16), vm((T, D), bf16), vm((T, D), bf16), vm((T, 128), f32),
         vm((T, 2 * QW), f32), vm((2, 2, T, 64), bf16), vm((2, T, 64), bf16), vm((2, T, 64), bf16),
         vm((2, 64, T), bf16), vm((2, 64, T), bf16), vm((2, 2, T, 64), bf16), vm((T, QW), bf16),
         vm((T, D), bf16), vm((2, RB, D), bf16), vm((RB, D), bf16), vm((RB, D), bf16), vm((RB, D), f32),
         vm((T, D), bf16), vm((T, 2 * F), bf16), vm((T, F), bf16),
         vm((T, 128), f32), vm((T, 128), f32), vm((area, RB), bf16), vm((2, 8, 2 * RB), f32),
         vm((T, QW), f32), vm((2, T, 64), f32), vm((2, T, 64), f32),
-        vm((T, 2 * CW), bf16), vm((T, CW), bf16), vm((T, CW), bf16), vm((RB, D), bf16), vm((T, CW), bf16),
+        vm((T, 2 * CW), bf16), vm((T, CW), bf16), vm((T, CW), bf16), vm((T, CW), bf16),
         vm((8, D), f32), vm((8, D), f32), vm((8, D), f32), vm((8, D), f32), vm((nz, 8, D), f32),
         sem((13,)), sem((7, nz)), sem((7, nz)), sem((7, nz)), sem((7, nz)),
         sem((8, nz)), sem((8, nz)), sem((8, nz)), sem((8, nz)),
         sem((4, 3)), sem((4, 3)), sem((3, 3)), sem((3, 3)), sem((nb, 3)), sem((nb, 3)), sem((3,)), sem((3,)),
-        sem((3,)), sem((3,)), sem((nz,)), sem((nz,)), sem((18,)),
+        sem((3,)), sem((3,)), sem((nz,)), sem((nz,)), sem((26,)),
     ]
     whole, hbm = pl.BlockSpec(memory_space=pltpu.VMEM), pl.BlockSpec(memory_space=pl.ANY)
     shape = jax.ShapeDtypeStruct
+    results = (
+        shape((T, CW), bf16), shape((T, CW), f32), shape((br, QW), f32), shape((br, KW), f32), shape((br, KW), f32),
+        shape((QW, br), f32), shape((br, F), f32), shape((br, F), f32), shape((F, br), f32),
+    )
     outs = pl.pallas_call(
         functools.partial(layer_kernel, nz),
-        out_shape=(
-            shape((T, CW), bf16), shape((T, CW), f32), shape((br, PW), f32), shape((br, F), f32),
-            shape((br, F), f32), shape((br, F), f32), shape((8, D), f32),
-        ),
+        out_shape=results + (shape((8, D), f32),),
         in_specs=[hbm, whole] + [hbm] * 7 + [whole] * 4 + [hbm],
-        out_specs=(hbm,) * 6 + (whole,),
+        out_specs=(hbm,) * 9 + (whole,),
         scratch_shapes=scratch,
         compiler_params=pltpu.CompilerParams(
             collective_id=0, has_side_effects=True, vmem_limit_bytes=64 * 2**20
         ),
         name="layer",
     )(
-        tokens, segment_ids, w_query, key_matrix, value_matrix, w_out.T, w_gate, w_up, w_down.T,
+        tokens, segment_ids, w_query, key_matrix, value_matrix, w_out, w_gate, w_up, w_down,
         norm_attn[None], norm_ffn[None], norm_query[None], norm_key[None], cotangent,
     )
-    layer_out, grad_tokens, g_attn, g_gate, g_up, g_down, gains = outs
-    return (
-        layer_out, grad_tokens, g_attn[:, :QW], g_attn[:, QW : QW + KW], g_attn[:, QW + KW : 2 * QW],
-        g_attn[:, 2 * QW :].T, g_gate, g_up, g_down.T, gains[0], gains[1],
-        gains[2, :64] + gains[2, 64:128], gains[2, 128:192] + gains[2, 192:256],
-    )
+    gain = shape((1, D), f32)
+    head_gain = shape((1, norm_query.shape[0]), f32)
+    outs = pl.pallas_call(
+        hand_out,
+        out_shape=results + (gain, gain, head_gain, head_gain),
+        in_specs=[pl.BlockSpec(memory_space=pltpu.HBM)] * 9 + [whole],
+        out_specs=(pl.BlockSpec(memory_space=pltpu.HBM),) * 9 + (whole,) * 4,
+        scratch_shapes=[vm(v.shape, v.dtype) for v in results] + [sem((2, 9))],
+        compiler_params=pltpu.CompilerParams(vmem_limit_bytes=63 * 2**20),
+        name="hand_out",
+    )(*outs)
+    return outs[:9] + tuple(v[0] for v in outs[9:])
 
 
 def solution(mesh):

time: 269 us -> 240 us (0.89); the launches traced: 266 us -> 240 us
  local copies, waits for them, and re-layouts: 14.2 us -> 0 us
  Pallas kernels: 250 us -> 239 us
    pallas_call x1 -> x2, Pallas kernels: 250 us -> 239 us  [the longest x1 235 us: per_device(): pl.pallas_call(functools.partial(layer_kernel, nz), out_shape=results + (...]
    unnamed x18 -> x0, local copies, waits for them, and re-layouts: 9.56 us -> none
    slice x2 -> x0, local copies, waits for them, and re-layouts: 2.96 us -> none  [the longest x1 1.53 us: per_device(): g_attn[:, QW + KW:2 * QW]]
where the time goes in v2:
time: 240 us
  Pallas kernels  239 us (100%)
    pallas_call x1, Pallas kernels, per_device(): pl.pallas_call(functools.partial(layer_kernel, nz), out_shape=results + (...  235 us

profile of v2, /device:TPU:0, one launch (start us, length us, event | category | flops | bytes accessed | tf_op | source)
XLA Modules:
  0.0 240.1 jit_solution(16140473952223480203)
XLA Ops:
  0.7 234.7 %layer.1 = (bf16[1024,256]{1,0:T(8,128)(2,1)}, f32[1024,256]{1,0:T(8,128)}, f32[128,256]{1,0:T(8,128)}, f32[128,128]{1,0:T(8,128)}, f32[128,128]{1,0:T(8,128)}, ...) custom-call(bf16[1024,256]{1,0:T(8,128)(2,1)} %tok_h.1, ...), custom_call_target="tpu_custom_call" | custom-call | tf_op jit(solution)/shard_map/layer/pallas_call | solution.py:871
  235.3 4.6 %hand_out.1 = (bf16[1024,256]{1,0:T(8,128)(2,1)}, f32[1024,256]{1,0:T(8,128)}, f32[128,256]{1,0:T(8,128)}, f32[128,128]{1,0:T(8,128)}, f32[128,128]{1,0:T(8,128)...) custom-call(bf16[1024,256]{1,0:T(8,128)(2,1)} %get-tuple-element.36., ...), custom_call_target="tpu_custom_call" | custom-call | tf_op jit(solution)/shard_map/hand_out/pallas_call | solution.py:887

commit v3 on v2

v3 whole, which is shorter than its diff:
```python
import functools
import math

import jax
import jax.numpy as jnp
from jax import lax
from jax.experimental import pallas as pl
from jax.experimental.pallas import tpu as pltpu
from jax.sharding import PartitionSpec as P

epsilon = 1e-05
rope_base = 1000000.0
longest = 512
ids = 8
f32, bf16 = jnp.float32, jnp.bfloat16
MESH = pl.DeviceIdType.MESH
RB = 256


def dot_nn(a, b):
    return lax.dot_general(a, b, (((1,), (0,)), ((), ())), preferred_element_type=f32)


def dot_nt(a, b):
    return lax.dot_general(a, b, (((1,), (1,)), ((), ())), preferred_element_type=f32)


def rows(i, n):
    return pl.ds(pl.multiple_of(i * n, n), n)


AG_PAIRS, RS_PAIRS = (5, 6), (0, 1)
ORDER = [
    ("owny", 0, "a"), ("gate_up", "a"), ("owny", 2, "a"), ("ownz", 0, "a"), ("owny", 1, "a"), ("fwd", 0, 1, "e"),
    ("ownz", 1, "a"), ("ownz", 2, "a"), ("toks", "a"), ("owny", 3, "a"), ("ownz", 3, "a"), ("fwd", 0, 1, "m"),
    ("fwd", 1, 1, "m"), ("cots", "a"), ("fwd", 1, 2, "m"), ("fwd", 0, 2, "m"), ("tables", "a"), ("fwd", 0, 3, "m"),
    ("owny", 4, "a"), ("fwd", 0, 2, "e"), ("fwd", 0, 3, "e"), ("ownz", 4, "a"), ("down", "a"), ("owny", 5, "a"),
    ("owny", 6, "a"), ("tokf", "a"), ("fwd", 1, 3, "m"), ("fwd", 2, 1, "m"), ("owny", 7, "a"), ("fwd", 3, 1, "m"),
    ("norm", "a"), ("fwd", 1, 1, "e"), ("fwd", 1, 2, "e"), ("fwd", 2, 2, "m"), ("project", "a"), ("fwd", 2, 3, "m"),
    ("att", 0, "a"), ("att", 1, "a"), ("fwd", 1, 3, "e"), ("fwd", 4, 1, "m"), ("fwd", 2, 1, "e"),
    ("fwd", 3, 2, "m"), ("cotf", "a"), ("ownz", 5, "a"), ("fwd", 3, 1, "e"), ("fwd", 3, 3, "m"), ("att", 2, "a"),
    ("ownz", 7, "a"), ("fwd", 2, 2, "e"), ("att", 3, "a"), ("aprod", "a"), ("fwd", 4, 2, "m"), ("fwd", 2, 3, "e"),
    ("ownz", 6, "a"), ("fwd", 6, 1, "e"), ("fwd", 5, 1, "m"), ("amid", "a"), ("aft", 0, "a"), ("fwd", 7, 1, "e"),
    ("fwd", 3, 2, "e"), ("fwd", 4, 3, "m"), ("fwd", 7, 1, "m"), ("fwd", 5, 2, "m"), ("aft", 1, "a"),
    ("fwd", 5, 1, "e"), ("fwd", 4, 1, "e"), ("fwd", 3, 3, "e"), ("fwd", 6, 1, "m"), ("fwd", 7, 2, "m"),
    ("nff", 0, "a"), ("fwd", 5, 2, "e"), ("fwd", 7, 3, "m"), ("fwd", 5, 3, "m"), ("fwd", 6, 2, "m"),
    ("nff", 1, "a"), ("fwd", 4, 2, "e"), ("fwd", 4, 3, "e"), ("ffn", 0, "a"), ("ffn", 1, "a"), ("fwd", 6, 2, "e"),
    ("fwd", 6, 3, "m"), ("fwd", 7, 2, "e"), ("wg", 0, "a"), ("wg", 1, "a"), ("fwd", 7, 3, "e"), ("ffn", 2, "a"),
    ("wg", 2, "a"), ("fwd", 5, 3, "e"), ("fwd", 6, 3, "e"), ("gh", 0, "a"), ("gh", 1, "a"), ("gh", 2, "a"),
    ("mid", 2, 0, "m"), ("wg", 3, "a"), ("gnfp", "a"), ("relay", 0, 0, "m"), ("gnfm", "a"), ("mid", 2, 0, "e"),
    ("mid", 3, 0, "e"), ("relay", 0, 1, "m"), ("mid", 3, 0, "m"), ("mid", 4, 0, "e"), ("naft", 0, "a"),
    ("mid", 4, 0, "m"), ("mid", 3, 1, "e"), ("mid", 4, 1, "e"), ("mid", 2, 1, "m"), ("mid", 5, 0, "m"),
    ("mid", 5, 0, "e"), ("naft", 1, "a"), ("relay", 3, 0, "m"), ("relay", 1, 0, "m"), ("mid", 2, 2, "m"),
    ("mid", 2, 1, "e"), ("mid", 3, 1, "m"), ("mid", 4, 1, "m"), ("mid", 3, 2, "m"), ("relay", 1, 1, "m"),
    ("relay", 4, 0, "m"), ("rlf", 0, "a"), ("mid", 3, 2, "e"), ("relay", 3, 1, "m"), ("rlf", 1, "a"),
    ("mid", 4, 2, "e"), ("mid", 2, 2, "e"), ("mid", 5, 1, "e"), ("relay", 2, 0, "m"), ("mid", 5, 1, "m"),
    ("gmix", "a"), ("brp", "a"), ("ab", 0, "a"), ("relay", 4, 1, "m"), ("relay", 2, 1, "m"), ("ab", 1, "a"),
    ("mid", 4, 2, "m"), ("wg", 6, "a"), ("brm", "a"), ("relay", 5, 0, "m"), ("mid", 5, 2, "m"), ("mid", 5, 2, "e"),
    ("ab", 2, "a"), ("ab", 3, "a"), ("pb", "a"), ("gnp", "a"), ("wg", 7, "a"), ("relay", 5, 1, "m"),
    ("mid", 6, 0, "m"), ("vc", "a"), ("gnm", "a"), ("mid", 6, 1, "m"), ("pre", 1, "e"), ("mid", 6, 0, "e"),
    ("mid", 7, 0, "e"), ("brf", "a"), ("pre", 1, "m"), ("mid", 7, 1, "e"), ("mid", 6, 1, "e"), ("fin", 5, "a"),
    ("mid", 7, 0, "m"), ("mid", 7, 1, "m"), ("mid", 7, 2, "e"), ("relay", 6, 0, "m"), ("relay", 7, 0, "m"),
    ("mid", 6, 2, "e"), ("mid", 7, 2, "m"), ("fin", 3, "a"), ("vx", "a"), ("mid", 6, 2, "m"), ("pre", 0, "m"),
    ("relay", 7, 1, "m"), ("pre", 0, "e"), ("relay", 6, 1, "m"), ("gnfin", "a"), ("vy", "a"), ("fin", 4, "a"),
    ("fin", 6, "a"), ("fin", 7, "a"), ("fin", 2, "a"), ("fin", 0, "a"), ("fin", 1, "a"), ("lof", "a"), ("end", "a"),
]


def layer_kernel(
    plan,
    tok_h, seg_ref, wq_h, wk_h, wv_h, wo_h, wg_h, wu_h, wd_h, ga_ref, gf_ref, gq_ref, gk_ref, cot_h,
    lo_h, gt_h, gquery_h, gkey_h, gvalue_h, gout_h, ggate_h, gup_h, gdown_h, gain_ref,
    W, WO, WD, GFO, GFD, G, RY, RZ, RYP, RZP, GF, Tk, Ct, Nm, R1, PRE, QS, KS, VS, KT, VT, DO, MX, PB, A0, B0, S0,
    RES, NF, GG, HID, CS, SN, BIAS, INV, DQ, DKV, AC, BC, SC, LOC, VEC, VC, VX, VY, VZ,
    loc_sem, agz_s, agz_r, agy_s, agy_r, rsy_s, rsy_r, rsz_s, rsz_r,
    cag_s, cag_r, crs_s, crs_r, gn_s, gn_r, lo_s, lo_r, vec_s, vec_r, vz_s, vz_r, out_sem,
):
    nz, tree, CH, RCH, ag_pairs, rs_pairs, place = plan
    T, D = Tk.shape
    br = RY.shape[1]
    QW, KW = PRE.shape[1] // 2, PRE.shape[1] // 4
    PW = 2 * QW + 2 * KW
    F = HID.shape[1]
    FC = F // 3
    HB = RB // 2
    down0 = PW + 2 * F
    nb = T // RB
    CW = D // 4
    GQ = GG.at[:, pl.ds(PW, 2 * QW)]
    PN = GG.at[:, pl.ds(PW + 2 * QW, D)]
    row, col = lax.axis_index("row"), lax.axis_index("col")
    z, y = row // 2, row % 2
    x, c = col // 2, col % 2
    ypeer = (row + 1 - 2 * y, col)
    cpeer = (row, col + 1 - 2 * c)
    xpeer = (row, (1 - x) * 2 + c)
    dpeer = (row, (1 - x) * 2 + 1 - c)
    partner = z + 1 - 2 * (z % 2)
    is_middle = (z == 1) | (z == 2)
    near, far = 2 - z // 2, 3 - 3 * (z // 2)

    def zdev(zz):
        return (zz * 2 + y, col)

    def zsrc(k):
        return [z, partner, near, far][k] if tree else (z + nz - k) % nz

    def zto(i):
        return [near, far, partner, z][i]

    def rc(src, dst, ss, rs, dev):
        return pltpu.make_async_remote_copy(
            src_ref=src, dst_ref=dst, send_sem=ss, recv_sem=rs, device_id=dev, device_id_type=MESH
        )

    def loop(n, body, first=0):
        def step(i, carry):
            body(i)
            return carry

        lax.fori_loop(first, n, step, 0)

    own = rows(row, br)
    mine = pl.ds(pl.multiple_of(col * CW, CW), CW)
    local = [
        (wq_h, W.at[own, pl.ds(0, QW)]),
        (wk_h, W.at[own, pl.ds(QW, KW)]),
        (wv_h, W.at[own, pl.ds(QW + KW, KW)]),
        (wo_h, WO),
        (tok_h, Tk.at[:, mine]),
        (cot_h, Ct.at[:, mine]),
    ]
    for j in range(3):
        local.append((wg_h.at[:, pl.ds(FC * j, FC)], W.at[own, pl.ds(PW + 2 * FC * j, FC)]))
        local.append((wu_h.at[:, pl.ds(FC * j, FC)], W.at[own, pl.ds(PW + 2 * FC * j + FC, FC)]))
    local.append((wd_h, WD))
    local = [pltpu.make_async_copy(s, d, loc_sem.at[i]) for i, (s, d) in enumerate(local)]

    def wblk(ch, zz, yy):
        start, width = CH[ch]
        return W.at[rows(zz * 2 + yy, br), pl.ds(start, width)]

    def wpair(ch, zz):
        start, width = CH[ch]
        return W.at[rows(zz, 2 * br), pl.ds(start, width)]

    def ag_z(ch, k, src, slot, dev):
        b = wpair(ch, src) if ch in ag_pairs else wblk(ch, src, y)
        return rc(b, b, agz_s.at[ch, k], agz_r.at[ch, slot], zdev(dev))

    def ag_y(ch, k, src, yy):
        b = wblk(ch, src, yy)
        return rc(b, b, agy_s.at[ch, k], agy_r.at[ch, k], ypeer)

    def own_y(ch):
        ag_y(ch, 0, z, y).start()

    def own_z(ch):
        if ch in ag_pairs:
            ag_y(ch, 0, z, 1 - y).wait_recv()
        if tree:
            ag_z(ch, 0, z, 1, partner).start()
            ag_z(ch, 1, z, jnp.where(is_middle, 2, 3), near).start()
        else:
            loop(nz, lambda k: ag_z(ch, k, z, k, (z + k) % nz).start(), 1)

    def forward(ch, k, middle):
        if not tree:
            if k == 3 and middle:

                def step(k):
                    ag_z(ch, k, zsrc(k), k, z).wait_recv()
                    ag_y(ch, k, zsrc(k), y).start()

                loop(nz, step, 1)
            return
        relayed = middle and k >= 2
        if ch in ag_pairs and not relayed:
            return
        ag_z(ch, k, zsrc(k), k, partner).wait_recv()
        if relayed:
            ag_z(ch, k, zsrc(k), k, partner).start()
        if ch not in ag_pairs:
            ag_y(ch, k, zsrc(k), y).start()

    def ag_wait(ch):
        if not tree:
            loop(nz, lambda k: ag_y(ch, k, zsrc(k), 1 - y).wait_recv())
        elif ch in ag_pairs:
            ag_z(ch, 0, partner, 1, partner).wait_recv()

            @pl.when(jnp.logical_not(is_middle))
            def _():
                ag_z(ch, 0, near, 2, partner).wait_recv()
                ag_z(ch, 0, far, 3, partner).wait_recv()

        else:
            for k in range(4):
                ag_y(ch, k, zsrc(k), 1 - y).wait_recv()

    def ag_done(ch):
        if not tree:
            loop(nz, lambda k: ag_y(ch, k, zsrc(k), y).wait_send())
            loop(nz, lambda k: ag_z(ch, k, z, k, z).wait_send(), 1)
            return
        for k in range(1 if ch in ag_pairs else 4):
            ag_y(ch, k, zsrc(k), y).wait_send()
        ag_z(ch, 0, z, 1, partner).wait_send()
        ag_z(ch, 1, z, 2, near).wait_send()

        @pl.when(is_middle)
        def _():
            ag_z(ch, 2, near, 2, partner).wait_send()
            ag_z(ch, 3, far, 3, partner).wait_send()

    def cag(n, block, parts=1):
        def copy(i, d, dev, h):
            return rc(block(d, h), block(d, h), cag_s.at[n, h, i], cag_r.at[n, h, i], dev)

        def start(h=0):
            copy(0, col, cpeer, h).start()
            copy(1, col, xpeer, h).start()

        def forward(h=0):
            copy(1, (1 - x) * 2 + c, xpeer, h).wait_recv()
            copy(2, (1 - x) * 2 + c, cpeer, h).start()

        def wait():
            for h in range(parts):
                copy(0, x * 2 + 1 - c, cpeer, h).wait_recv()
                copy(2, (1 - x) * 2 + 1 - c, cpeer, h).wait_recv()

        def done():
            for h in range(parts):
                copy(0, col, cpeer, h).wait_send()
                copy(1, col, xpeer, h).wait_send()
                copy(2, (1 - x) * 2 + c, cpeer, h).wait_send()

        return start, forward, wait, done

    def col_block(ref):
        return lambda d, h: ref.at[:, pl.ds(pl.multiple_of(d * CW, CW), CW)]

    def row_block(ref):
        return lambda d, h: ref.at[rows(d * 2 + h, HB), :]

    tok_start, tok_forward, tok_wait, tok_done = cag(0, col_block(Tk))
    cot_start, cot_forward, cot_wait, cot_done = cag(1, col_block(Ct))
    nf_start, nf_forward, nf_wait, nf_done = cag(2, row_block(NF), 2)
    rl_start, rl_forward, rl_wait, rl_done = cag(3, row_block(Ct), 2)

    def crs(n, A, B, S):
        def to_core(i, xx, cc):
            return rc(PB.at[rows(xx * 2 + cc, RB), :], A(xx), crs_s.at[n, i], crs_r.at[n, i], cpeer)

        def to_x(h):
            half = rows(h, HB)
            return rc(S.at[half, :], B.at[half, :], crs_s.at[n, 2 + h], crs_r.at[n, 2 + h], xpeer)

        def produce(part):
            def step(i):
                xx = jnp.where(i < 2, 1 - x, x)
                cc = jnp.where(i % 2 == 0, 1 - c, c)
                PB[rows(xx * 2 + cc, RB), :] = part(xx * 2 + cc).astype(bf16)

                @pl.when(i % 2 == 0)
                def _():
                    to_core(i // 2, xx, 1 - c).start()

            loop(4, step)

        def middle():
            to_core(0, 1 - x, c).wait_recv()

            def step(i):
                r = rows(i, 32)
                block = PB[pl.ds(pl.multiple_of(((1 - x) * 2 + c) * RB + i * 32, 32), 32), :]
                S[r, :] = (block.astype(f32) + A(1 - x)[r, :].astype(f32)).astype(bf16)

            for h in range(2):
                loop(HB // 32 * (h + 1), step, HB // 32 * h)
                to_x(h).start()

        def total(h, use):
            if h == 0:
                to_core(1, x, c).wait_recv()
            to_x(h).wait_recv()

            def step(i):
                r = rows(i, 32)
                at = pl.ds(pl.multiple_of(col * RB + i * 32, 32), 32)
                use(r, at, PB[at, :].astype(f32) + A(x)[r, :].astype(f32) + B[r, :].astype(f32))

            loop(HB // 32 * (h + 1), step, HB // 32 * h)

        def done():
            to_core(0, 1 - x, 1 - c).wait_send()
            to_core(1, x, 1 - c).wait_send()
            to_x(0).wait_send()
            to_x(1).wait_send()

        return produce, middle, total, done

    a_produce, a_middle, a_total, a_done = crs(0, lambda i: A0.at[i], B0, S0)
    n_produce, n_middle, n_total, n_done = crs(1, lambda i: A0.at[i], B0, S0)
    b_produce, b_middle, b_total, b_done = crs(
        2, lambda i: NF.at[rows(i, RB), :], NF.at[pl.ds(2 * RB, RB), :], NF.at[pl.ds(3 * RB, RB), :]
    )

    def gcol(ch):
        start, width = RCH[ch]
        return (G, start - PW, width) if start >= PW else (GG, start, width)

    def gblk(ch, zz, yy):
        ref, start, width = gcol(ch)
        return ref.at[rows(zz * 2 + yy, br), pl.ds(start, width)]

    def part_of(ch):
        return pl.ds(place[ch], RCH[ch][1])

    def rs_y(ch, zz, yy):
        landing = RYP.at[:, part_of(ch)] if ch in rs_pairs else RY.at[zz, :, part_of(ch)]
        return rc(gblk(ch, zz, yy), landing, rsy_s.at[ch, zz], rsy_r.at[ch, zz], ypeer)

    def rs_z(ch, k, zz, slot, dev):
        if ch in rs_pairs:
            ref, start, width = gcol(ch)
            src, dst = ref.at[rows(zz, 2 * br), pl.ds(start, width)], RZP.at[slot, :, part_of(ch)]
        else:
            src, dst = RY.at[zz, :, part_of(ch)], RZ.at[slot, :, part_of(ch)]
        return rc(src, dst, rsz_s.at[ch, k], rsz_r.at[ch, slot], zdev(dev))

    zper = RB // (2 * br)

    def weight_grad(left, pieces):
        def one(i, d):
            lt = jnp.transpose(left[:, rows(d, RB)])
            for ch, right in pieces:
                ref, start, width = gcol(ch)
                ref[rows(d, RB), pl.ds(start, width)] = dot_nn(lt, right[...]).astype(bf16)
                if ch not in rs_pairs:
                    loop(zper, lambda s: rs_y(ch, d * zper + s, 1 - y).start())
                elif i == 2:
                    rs_z(ch, 2, d, 2, partner).start()
                elif i < 2:

                    @pl.when(jnp.logical_not(is_middle))
                    def _():
                        rs_z(ch, i, d, i, partner).start()

        if any(ch in rs_pairs for ch, _ in pieces):
            for i in range(4):
                one(i, zto(i))
        elif tree:

            def step(i):
                one(i, jnp.where(i == 0, near, jnp.where(i == 1, far, jnp.where(i == 2, partner, z))))

            loop(4, step)
        else:
            loop(D // RB, lambda i: one(i, (row * br // RB + 1 + i) % (D // RB)))

    def rs_mid(ch, i, middle):
        ref, gstart, width = gcol(ch)

        def one(zz):
            rs_y(ch, zz, y).wait_recv()

            def add(j):
                r = rows(j, 16)
                g = ref[pl.ds(pl.multiple_of((zz * 2 + y) * br + j * 16, 16), 16), pl.ds(gstart, width)]
                t = RY[zz, r, part_of(ch)]
                RY[zz, r, part_of(ch)] = (g.astype(f32) + t.astype(f32)).astype(bf16)

            loop(br // 16, add)

        if not tree:
            if i == 2 and middle:

                def step(k):
                    zz = (z + k) % nz
                    one(zz)
                    rs_z(ch, k, zz, k - 1, zz).start()

                loop(nz, step, 1)
        elif ch not in rs_pairs:
            one(zto(i))
            if i == 2 or not middle:
                rs_z(ch, i, zto(i), i, partner).start()

    def rs_relay(ch, i):
        if not tree:
            return
        zz = zto(i)
        rs_z(ch, i, zz, i, partner).wait_recv()
        ref, gstart, width = gcol(ch)

        def add(j):
            r = rows(j, 16)
            if ch in rs_pairs:
                at = pl.ds(pl.multiple_of(zz * 2 * br + j * 16, 16), 16)
                t = ref[at, pl.ds(gstart, width)].astype(f32) + RZP[i, r, part_of(ch)].astype(f32)
                ref[at, pl.ds(gstart, width)] = t.astype(bf16)
            else:
                t = RY[zz, r, part_of(ch)].astype(f32) + RZ[i, r, part_of(ch)].astype(f32)
                RY[zz, r, part_of(ch)] = t.astype(bf16)

        loop((2 * br if ch in rs_pairs else br) // 16, add)
        rs_z(ch, i, zz, 3, zz).start()

    def rs_pre(ch):
        if ch not in rs_pairs:
            return
        for slot in (2, 3):
            rs_z(ch, 2, z, slot, partner).wait_recv()
        ref, gstart, width = gcol(ch)

        def add(j):
            at = pl.ds(pl.multiple_of((z * 2 + 1 - y) * br + j * 16, 16), 16)
            r = pl.ds(pl.multiple_of((1 - y) * br + j * 16, 16), 16)
            t = ref[at, pl.ds(gstart, width)].astype(f32)
            t = t + RZP[2, r, part_of(ch)].astype(f32) + RZP[3, r, part_of(ch)].astype(f32)
            ref[at, pl.ds(gstart, width)] = t.astype(bf16)

        loop(br // 16, add)
        rs_y(ch, z, 1 - y).start()

    def outs(ch):
        start, width = RCH[ch]
        if start >= down0:
            pairs = [(GFD.at[pl.ds(start - down0, width), :], gdown_h.at[pl.ds(start - down0, width), :])]
        elif start >= PW:
            at = pl.ds((start - PW) // 2, FC)
            pairs = [
                (GF.at[:, pl.ds(start - 2 * KW, FC)], ggate_h.at[:, at]),
                (GF.at[:, pl.ds(start - 2 * KW + FC, FC)], gup_h.at[:, at]),
            ]
        elif start == 2 * QW:
            pairs = [(GFO, gout_h)]
        else:
            pairs = [
                (GF.at[:, pl.ds(0, QW)], gquery_h),
                (GF.at[:, pl.ds(QW, KW)], gkey_h),
                (GF.at[:, pl.ds(QW + KW, KW)], gvalue_h),
            ]
        return [pltpu.make_async_copy(a, b, out_sem.at[3 * ch + i]) for i, (a, b) in enumerate(pairs)]

    def rs_fin(ch):
        ref, gstart, width = gcol(ch)
        start = RCH[ch][0]
        paired = ch in rs_pairs
        rs_y(ch, z, y).wait_recv()
        if not tree:
            loop(nz - 1, lambda k: rs_z(ch, 0, z, k, z).wait_recv())
        elif not paired:
            for slot in (2, 3):
                rs_z(ch, 0, z, slot, z).wait_recv()

        def total(r0, rn, c0, cn):
            r = pl.ds(r0, rn)
            g = ref[pl.ds(pl.multiple_of(row * br + r0, 16), rn), pl.ds(gstart + c0, cn)]
            part = pl.ds(place[ch] + c0, cn)
            if paired:
                rp = pl.ds(pl.multiple_of(y * br + r0, 16), rn)
                t = RZP[2, rp, part].astype(f32) + RZP[3, rp, part].astype(f32)
                return g.astype(f32) + t + RYP[r, part].astype(f32)
            t = g.astype(f32) + RY[z, r, part].astype(f32)
            if tree:
                return t + (RZ[2, r, part].astype(f32) + RZ[3, r, part].astype(f32))
            return lax.fori_loop(0, nz - 1, lambda k, t: t + RZ[k, r, part].astype(f32), t)

        if start >= down0 or start == 2 * QW:
            for c0 in range(0, width, 128):
                t = jnp.transpose(total(0, br, c0, 128))
                if start >= down0:
                    GFD[pl.ds(start - down0 + c0, 128), :] = t
                else:
                    GFO[pl.ds(c0, 128), :] = t
        else:
            at = start - 2 * KW if start >= PW else start

            def add(i):
                r0 = pl.multiple_of(i * 16, 16)
                GF[pl.ds(r0, 16), pl.ds(at, width)] = total(r0, 16, 0, width)

            loop(br // 16, add)
        for copy in outs(ch):
            copy.start()

    def rs_done(ch):
        if ch in rs_pairs:
            rs_y(ch, z, 1 - y).wait_send()
        else:
            loop(nz, lambda zz: rs_y(ch, zz, 1 - y).wait_send())
        if tree:
            for i in range(3):
                rs_z(ch, i, zto(i), 0, partner).wait_send()
        else:
            loop(nz, lambda k: rs_z(ch, k, z, 0, z).wait_send(), 1)
        for copy in outs(ch):
            copy.wait()

    for copy in local:
        copy.start()
    bar = pltpu.get_barrier_semaphore()
    for dev in (ypeer, cpeer, xpeer, dpeer):
        pl.semaphore_signal(bar, inc=1, device_id=dev, device_id_type=MESH)

    def greet(k):
        pl.semaphore_signal(bar, inc=1, device_id=zdev((z + k) % nz), device_id_type=MESH)

    loop(nz, greet, 1)
    for i in range(4):
        local[i].wait()
    W[own, pl.ds(2 * QW, QW)] = jnp.transpose(WO[...])
    pl.semaphore_wait(bar, 4 + nz - 1)

    def load_gate_up():
        for i in range(6, 12):
            local[i].wait()

    def load_down():
        local[12].wait()
        W[own, pl.ds(down0, F)] = jnp.transpose(WD[...])

    def start_tokens():
        local[4].wait()
        tok_start()

    def start_cotangent():
        local[5].wait()
        cot_start()

    lane = lax.broadcasted_iota(jnp.int32, (1, 128), 1)
    gain_q = jnp.concatenate([gq_ref[...], gq_ref[...]], axis=1)
    gain_k = jnp.concatenate([gk_ref[...], gk_ref[...]], axis=1)
    windows = []
    for i in range(nb):
        start = max(0, RB * i - longest)
        windows.append((start, RB * (i + 1) - start, sum(w for _, w, _ in windows)))

    def tables():
        VEC[...] = jnp.zeros(VEC.shape, f32)
        seg = seg_ref[...]
        first = jnp.zeros((1, T), jnp.int32)
        for d in range(ids):
            count = jnp.sum((seg == d).astype(f32), axis=1, keepdims=True).astype(jnp.int32)
            first = first + jnp.where(seg > d, count, 0)
        place = lax.broadcasted_iota(jnp.int32, (1, T), 1)
        inverse_freq = jnp.exp((lane % 32).astype(f32) * (-2.0 / 64 * math.log(rope_base)))
        CS[...] = jnp.transpose(jnp.broadcast_to((place - first).astype(f32), (128, T)))

        def fill(i):
            angle = CS[rows(i, 128), :] * inverse_freq
            sine = jnp.sin(angle)
            CS[rows(i, 128), :] = jnp.cos(angle)
            SN[rows(i, 128), :] = jnp.where(lane % 64 < 32, -sine, sine)

        loop(T // 128, fill)
        for i, (start, width, at) in enumerate(windows):
            key_place = lax.broadcasted_iota(jnp.int32, (width, RB), 0) + start
            q_place, q_first = place[:, RB * i : RB * (i + 1)], first[:, RB * i : RB * (i + 1)]
            seen = (key_place <= q_place) & (key_place >= q_first)
            BIAS[pl.ds(at, width), :] = jnp.where(seen, 0.0, -1e30).astype(bf16)

    def head_mean(v):
        half_a = lax.broadcasted_iota(jnp.int32, (128, 128), 0) // 64
        half_b = lax.broadcasted_iota(jnp.int32, (128, 128), 1) // 64
        mean_matrix = jnp.where(half_a == half_b, 1.0 / 64, 0.0).astype(bf16)
        high = v.astype(bf16)
        low = (v - high.astype(f32)).astype(bf16)
        return dot_nn(high, mean_matrix) + dot_nn(low, mean_matrix)

    def turn(v):
        return jnp.where(lane % 64 < 32, pltpu.roll(v, 96, 1), pltpu.roll(v, 32, 1))

    def norm_tokens():
        tok_wait()

        def step(i):
            t = Tk[rows(i, 128), :].astype(f32)
            r = lax.rsqrt(jnp.mean(t * t, axis=1, keepdims=True) + epsilon)
            R1[rows(i, 128), :] = jnp.broadcast_to(r, (128, 128))
            Nm[rows(i, 128), :] = (t * r * ga_ref[...]).astype(bf16)

        loop(T // 128, step)

    def project():
        ag_wait(0)

        def step(i):
            r = rows(i, RB)
            PRE[r, :] = dot_nn(Nm[r, :], W[:, pl.ds(0, 2 * QW)])
            cos, sin = CS[r, :], SN[r, :]
            for p in range(3):
                v = PRE[r, pl.ds(128 * p, 128)]
                n = v * lax.rsqrt(head_mean(v * v) + epsilon)
                u = n * (gain_q if p < 2 else gain_k)
                u = (u * cos + turn(u) * sin).astype(bf16)
                if p < 2:
                    u = u * jnp.asarray(0.125, bf16)
                    QS[p, 0, r, :] = u[:, :64]
                    QS[p, 1, r, :] = u[:, 64:]
                else:
                    KS[0, r, :] = u[:, :64]
                    KS[1, r, :] = u[:, 64:]
                    ut = jnp.transpose(u)
                    KT[0, :, r] = ut[:64, :]
                    KT[1, :, r] = ut[64:, :]
            v = PRE[r, pl.ds(384, 128)].astype(bf16)
            VS[0, r, :] = v[:, :64]
            VS[1, r, :] = v[:, 64:]
            vt = jnp.transpose(v)
            VT[0, :, r] = vt[:64, :]
            VT[1, :, r] = vt[64:, :]

        loop(nb, step)

    def attend(i):
        start, width, at = windows[i]
        keys = pl.ds(start, width)
        r = pl.ds(RB * i, RB)

        def step(h):
            q = QS[h, :, r, :].reshape(2 * RB, 64)
            bias = BIAS[pl.ds(at, width), :].astype(f32)
            s = dot_nt(KS[h, keys, :], q) + jnp.concatenate([bias, bias], axis=1)
            e = jnp.exp(s)
            inv = 1.0 / jnp.sum(e, axis=0, keepdims=True)
            INV[h, pl.ds(i, 1), :] = inv
            o = dot_nn(VT[h, :, keys], (e * inv).astype(bf16))
            o = jnp.concatenate([o[:, :RB], o[:, RB:]], axis=0)
            MX[r, pl.ds(pl.multiple_of(h * 128, 128), 128)] = jnp.transpose(o).astype(bf16)

        loop(2, step)

    def attention_out():
        ag_wait(1)
        a_produce(lambda d: dot_nt(MX[rows(d, RB), :], W[:, pl.ds(2 * QW, QW)]))

    def after_attention(h):
        def use(r, at, summed):
            v = Tk[at, :].astype(f32) + summed
            RES[r, :] = v
            n = v * lax.rsqrt(jnp.mean(v * v, axis=1, keepdims=True) + epsilon)
            NF[at, :] = (n * gf_ref[...]).astype(bf16)

        a_total(h, use)
        nf_start(h)

    def ffn(j):
        if j == 0:
            nf_wait()
            nf_done()
            a_done()
        ag_wait(2 + j)

        def step(i):
            r = rows(i, RB)
            n = NF[r, :]
            gate = dot_nn(n, W[:, pl.ds(PW + 2 * FC * j, FC)])
            up = dot_nn(n, W[:, pl.ds(PW + 2 * FC * j + FC, FC)])
            sig = 1.0 / (1.0 + jnp.exp(-gate))
            act = gate * sig
            HID[r, pl.ds(FC * j, FC)] = (act * up).astype(bf16)
            GG[r, pl.ds(2 * FC * j, FC)] = (up * (sig + act * (1.0 - sig))).astype(bf16)
            GG[r, pl.ds(2 * FC * j + FC, FC)] = act.astype(bf16)

        loop(nb, step)

    def grad_weights(what):
        if what < 3:
            if what == 0:
                cot_wait()
                cot_done()
            weight_grad(Ct, [(what, HID.at[:, pl.ds(FC * what, FC)])])
        elif what == 3:
            weight_grad(NF, [(3 + j, GG.at[:, pl.ds(2 * FC * j, 2 * FC)]) for j in range(3)])
        elif what == 6:
            weight_grad(Ct, [(6, MX)])
        else:
            weight_grad(Nm, [(7, GQ)])

    def grad_hidden(j):
        ag_wait(5 + j)

        def step(i):
            r = rows(i, RB)
            gh = dot_nn(Ct[r, :], W[:, pl.ds(down0 + FC * j, FC)])
            a, b = pl.ds(2 * FC * j, FC), pl.ds(2 * FC * j + FC, FC)
            GG[r, a] = (gh * GG[r, a].astype(f32)).astype(bf16)
            GG[r, b] = (gh * GG[r, b].astype(f32)).astype(bf16)

        loop(nb, step)

    def grad_ffn_norm():
        n_produce(lambda d: dot_nt(GG[rows(d, RB), :], W[:, pl.ds(PW, 2 * F)]))

    def after_ffn(h):
        def use(r, at, gy):
            v = RES[r, :]
            inv = lax.rsqrt(jnp.mean(v * v, axis=1, keepdims=True) + epsilon)
            n = v * inv
            VEC[1:2, :] += jnp.sum(gy * n, axis=0, keepdims=True)
            g = gy * gf_ref[...]
            g = inv * (g - n * jnp.mean(g * n, axis=1, keepdims=True))
            Ct[at, :] = (Ct[at, :].astype(f32) + g).astype(bf16)

        n_total(h, use)
        rl_start(h)

    def grad_mixed():
        rl_wait()
        DKV[...] = jnp.zeros(DKV.shape, f32)

        def step(i):
            r = rows(i, RB)
            g = dot_nn(Ct[r, :], W[:, pl.ds(2 * QW, QW)]).astype(bf16)
            for p in range(2):
                DO[p, 0, r, :] = g[:, 128 * p : 128 * p + 64]
                DO[p, 1, r, :] = g[:, 128 * p + 64 : 128 * p + 128]

        loop(nb, step)

    def attend_back(i):
        start, width, at = windows[i]
        keys = pl.ds(start, width)
        r = pl.ds(RB * i, RB)

        def step(h):
            q = QS[h, :, r, :].reshape(2 * RB, 64)
            do = DO[h, :, r, :].reshape(2 * RB, 64)
            bias = BIAS[pl.ds(at, width), :].astype(f32)
            s = dot_nt(KS[h, keys, :], q) + jnp.concatenate([bias, bias], axis=1)
            p = jnp.exp(s) * INV[h, pl.ds(i, 1), :]
            dp = dot_nt(VS[h, keys, :], do)
            ds = (p * (dp - jnp.sum(p * dp, axis=0, keepdims=True))).astype(bf16)
            DKV[h, keys, :] += jnp.concatenate([dot_nn(ds, q), dot_nn(p.astype(bf16), do)], axis=1)
            g = dot_nn(KT[h, :, keys], ds) * 0.125
            g = jnp.concatenate([g[:, :RB], g[:, RB:]], axis=0)
            DQ[r, pl.ds(pl.multiple_of(h * 128, 128), 128)] = jnp.transpose(g)

        loop(2, step)

    def project_back():
        def step(i):
            r = rows(i, RB)
            cos, sin = CS[r, :], SN[r, :]
            for p in range(3):
                if p < 2:
                    g = DQ[r, pl.ds(128 * p, 128)]
                else:
                    g = jnp.concatenate([DKV[0, r, pl.ds(0, 64)], DKV[1, r, pl.ds(0, 64)]], axis=1)
                g = g * cos - turn(g) * sin
                v = PRE[r, pl.ds(128 * p, 128)]
                inv = lax.rsqrt(head_mean(v * v) + epsilon)
                n = v * inv
                s = pl.ds(0 if p < 2 else 128, 128)
                VEC[2:3, s] += jnp.sum(g * n, axis=0, keepdims=True)
                g = g * (gain_q if p < 2 else gain_k)
                GQ[r, pl.ds(128 * p, 128)] = (inv * (g - n * head_mean(g * n))).astype(bf16)
            v = jnp.concatenate([DKV[0, r, pl.ds(64, 64)], DKV[1, r, pl.ds(64, 64)]], axis=1)
            GQ[r, pl.ds(384, 128)] = v.astype(bf16)

        loop(nb, step)

    def gn_core(i, k, xx, cc):
        return rc(
            PN.at[rows(i, RB), pl.ds(pl.multiple_of((xx * 2 + cc) * CW, CW), CW)],
            AC.at[rows(i, RB), pl.ds(pl.multiple_of(xx * CW, CW), CW)],
            gn_s.at[i, k], gn_r.at[i, k], cpeer,
        )

    def gn_x(i):
        return rc(SC.at[rows(i, RB), :], BC.at[rows(i, RB), :], gn_s.at[i, 2], gn_r.at[i, 2], xpeer)

    vec_c = rc(VEC, VC, vec_s.at[0], vec_r.at[0], cpeer)
    vec_x = rc(VEC, VX, vec_s.at[1], vec_r.at[1], xpeer)
    vec_y = rc(VEC, VY, vec_s.at[2], vec_r.at[2], ypeer)

    def vz_copy(k, src):
        return rc(VZ.at[src], VZ.at[src], vz_s.at[k], vz_r.at[k], zdev((z + k) % nz))

    def gn_produce():
        def step(i):
            r = rows(i, RB)
            g = dot_nt(GQ[r, :], W[:, pl.ds(0, 2 * QW)])
            PN[r, :] = g.astype(bf16)
            gn_core(i, 0, 1 - x, 1 - c).start()
            gn_core(i, 1, x, 1 - c).start()
            g = g * (Tk[r, :].astype(f32) * R1[r, pl.ds(0, 1)])
            VEC[0:1, :] += jnp.sum(g, axis=0, keepdims=True)
            s = jnp.sum(g * ga_ref[...], axis=1, keepdims=True)
            VEC[3:4, r] = jnp.transpose(jnp.broadcast_to(s, (RB, 128)))[0:1, :]

        loop(nb, step)
        vec_c.start()

    def gn_middle():
        def step(i):
            r = rows(i, RB)
            gn_core(i, 0, 1 - x, c).wait_recv()
            a = PN[r, pl.ds(pl.multiple_of(((1 - x) * 2 + c) * CW, CW), CW)].astype(f32)
            b = AC[r, pl.ds(pl.multiple_of((1 - x) * CW, CW), CW)].astype(f32)
            SC[r, :] = (a + b).astype(bf16)
            gn_x(i).start()

        loop(nb, step)

    def vec_step(copy, landing, following):
        copy.wait_recv()
        copy.wait_send()
        VEC[...] += landing[...]
        following.start()

    def vec_last():
        vec_y.wait_recv()
        vec_y.wait_send()
        VZ[z] = VEC[...] + VY[...]
        loop(nz, lambda k: vz_copy(k, z).start(), 1)

    gt_copy = pltpu.make_async_copy(DQ, gt_h, out_sem.at[24])
    lo_out = pltpu.make_async_copy(LOC, lo_h, out_sem.at[25])

    def gn_finish():
        def step(i):
            r = rows(i, RB)
            gn_core(i, 1, x, c).wait_recv()
            gn_x(i).wait_recv()
            g = PN[r, mine].astype(f32) + AC[r, pl.ds(pl.multiple_of(x * CW, CW), CW)].astype(f32)
            g = (g + BC[r, :].astype(f32)) * ga_ref[:, mine]
            inv = R1[r, pl.ds(0, 1)]
            s = jnp.transpose(jnp.broadcast_to(VEC[3:4, r], (128, RB)))[:, 0:1] * (1.0 / D)
            n = Tk[r, mine].astype(f32) * inv
            DQ[r, :] = Ct[r, mine].astype(f32) + inv * (g - n * s)

        loop(nb, step)
        gt_copy.start()

    others = [(0, x * 2 + 1 - c, cpeer), (1, (1 - x) * 2 + c, xpeer), (2, (1 - x) * 2 + 1 - c, dpeer)]

    def lo_copy(i, d, dev):
        return rc(
            S0.at[:, pl.ds(pl.multiple_of(d * CW, CW), CW)], LOC.at[rows(col, RB), :], lo_s.at[i], lo_r.at[i], dev
        )

    def branch():
        n_done()
        b_produce(lambda d: dot_nt(HID[rows(d, RB), :], W[:, pl.ds(down0, F)]))

    def block_out():
        def use(r, at, summed):
            S0[r, :] = (RES[r, :] + summed).astype(bf16)

        b_total(0, use)
        b_total(1, use)
        for i, d, dev in others:
            lo_copy(i, d, dev).start()
        LOC[rows(col, RB), :] = S0[:, mine]

    def block_out_wait():
        for i, d, dev in others:
            lo_copy(i, d, dev).wait_recv()
        lo_out.start()

    def finish():
        loop(nz, lambda k: vz_copy(k, (z + nz - k) % nz).wait_recv(), 1)
        gain_ref[...] = lax.fori_loop(1, nz, lambda k, t: t + VZ[k], VZ[0])
        tok_done()
        rl_done()
        b_done()
        for i, d, dev in others:
            lo_copy(i, d, dev).wait_send()

        def gn_done(i):
            gn_core(i, 0, 1 - x, 1 - c).wait_send()
            gn_core(i, 1, x, 1 - c).wait_send()
            gn_x(i).wait_send()

        loop(nb, gn_done)
        loop(nz, lambda k: vz_copy(k, z).wait_send(), 1)
        for ch in range(len(CH)):
            ag_done(ch)
        for ch in range(len(RCH)):
            rs_done(ch)
        gt_copy.wait()
        lo_out.wait()

    steps = {
        "gate_up": load_gate_up, "down": load_down, "toks": start_tokens, "cots": start_cotangent,
        "owny": own_y, "ownz": own_z, "fwd": forward, "tokf": tok_forward, "cotf": cot_forward,
        "tables": tables, "norm": norm_tokens, "project": project, "att": attend, "aprod": attention_out,
        "amid": a_middle, "aft": after_attention, "nff": nf_forward, "ffn": ffn, "wg": grad_weights,
        "gh": grad_hidden, "gnfp": grad_ffn_norm, "gnfm": n_middle, "naft": after_ffn, "rlf": rl_forward,
        "gmix": grad_mixed, "ab": attend_back, "pb": project_back, "gnp": gn_produce, "gnm": gn_middle,
        "vc": lambda: vec_step(vec_c, VC, vec_x), "vx": lambda: vec_step(vec_x, VX, vec_y), "vy": vec_last,
        "gnfin": gn_finish, "brp": branch, "brm": b_middle, "brf": block_out, "lof": block_out_wait,
        "mid": rs_mid, "relay": rs_relay, "pre": rs_pre, "fin": rs_fin, "end": finish,
    }
    for name, *which, who in ORDER:
        if name in ("fwd", "mid"):
            run = functools.partial(steps[name], *which, who == "m")
        else:
            run = functools.partial(steps[name], *which)
        if who == "a" or not tree:
            if who != "e" or name in ("fwd", "mid"):
                run()
        else:

            @pl.when(is_middle if who == "m" else jnp.logical_not(is_middle))
            def _():
                run()


def hand_out(*refs):
    sources, gains, targets, held, sem = refs[:9], refs[9], refs[10:19], refs[23:32], refs[32]
    loads = [pltpu.make_async_copy(a, b, sem.at[0, i]) for i, (a, b) in enumerate(zip(sources, held))]
    stores = [pltpu.make_async_copy(a, b, sem.at[1, i]) for i, (a, b) in enumerate(zip(held, targets))]
    for copy in loads:
        copy.start()
    attn, ffn, query, key = refs[19:23]
    attn[...] = gains[0:1, :]
    ffn[...] = gains[1:2, :]
    query[...] = gains[2:3, 0:64] + gains[2:3, 64:128]
    key[...] = gains[2:3, 128:192] + gains[2:3, 192:256]
    for load, store in zip(loads, stores):
        load.wait()
        store.start()
    for store in stores:
        store.wait()


def per_device(
    n_row, tokens, segment_ids, w_query, key_matrix, value_matrix, w_out, w_gate, w_up, w_down,
    norm_attn, norm_ffn, norm_query, norm_key, cotangent,
):
    T, CW = tokens.shape
    br, QW = w_query.shape
    KW = key_matrix.shape[1]
    F = w_gate.shape[1]
    D = br * n_row
    nz = n_row // 2
    PW = 2 * QW + 2 * KW
    WW = PW + 3 * F
    FC = F // 3
    nb = T // RB
    area = sum(RB * (i + 1) - max(0, RB * i - longest) for i in range(nb))
    chunks = [(0, 2 * QW), (2 * QW, QW)]
    chunks += [(PW + 2 * FC * j, 2 * FC) for j in range(3)] + [(PW + 2 * F + FC * j, FC) for j in range(3)]
    grads = chunks[5:8] + chunks[2:5] + [chunks[1], chunks[0]]
    tree = nz == 4
    ag_pairs, rs_pairs = (AG_PAIRS, RS_PAIRS) if tree else ((), ())
    place, widths = [], [0, 0]
    for ch, (_, width) in enumerate(grads):
        paired = ch in rs_pairs
        place.append(widths[paired])
        widths[paired] += width
    plan = (nz, tree, chunks, grads, ag_pairs, rs_pairs, place)
    single, paired = widths[0], max(widths[1], 128)
    slots = 4 if tree else nz - 1
    vm, sem = pltpu.VMEM, pltpu.SemaphoreType.DMA
    scratch = [
        vm((D, WW), bf16), vm((QW, br), bf16), vm((F, br), bf16), vm((QW, br), f32), vm((F, br), f32),
        vm((D, 3 * F), bf16), vm((nz, br, single), bf16), vm((slots, br, single), bf16),
        vm((br, paired), bf16), vm((4, 2 * br, paired), bf16),
        vm((br, 2 * QW + 2 * F), f32), vm((T, D), bf16), vm((T, D), bf16), vm((T, D), bf16), vm((T, 128), f32),
        vm((T, 2 * QW), f32), vm((2, 2, T, 64), bf16), vm((2, T, 64), bf16), vm((2, T, 64), bf16),
        vm((2, 64, T), bf16), vm((2, 64, T), bf16), vm((2, 2, T, 64), bf16), vm((T, QW), bf16),
        vm((T, D), bf16), vm((2, RB, D), bf16), vm((RB, D), bf16), vm((RB, D), bf16), vm((RB, D), f32),
        vm((T, D), bf16), vm((T, 2 * F), bf16), vm((T, F), bf16),
        vm((T, 128), f32), vm((T, 128), f32), vm((area, RB), bf16), vm((2, 8, 2 * RB), f32),
        vm((T, QW), f32), vm((2, T, 128), f32),
        vm((T, 2 * CW), bf16), vm((T, CW), bf16), vm((T, CW), bf16), vm((T, CW), bf16),
        vm((8, D), f32), vm((8, D), f32), vm((8, D), f32), vm((8, D), f32), vm((nz, 8, D), f32),
        sem((13,)), sem((8, nz)), sem((8, nz)), sem((8, nz)), sem((8, nz)),
        sem((8, nz)), sem((8, nz)), sem((8, nz)), sem((8, nz)),
        sem((4, 2, 3)), sem((4, 2, 3)), sem((3, 4)), sem((3, 4)), sem((nb, 3)), sem((nb, 3)), sem((3,)), sem((3,)),
        sem((3,)), sem((3,)), sem((nz,)), sem((nz,)), sem((26,)),
    ]
    whole, hbm = pl.BlockSpec(memory_space=pltpu.VMEM), pl.BlockSpec(memory_space=pl.ANY)
    shape = jax.ShapeDtypeStruct
    results = (
        shape((T, CW), bf16), shape((T, CW), f32), shape((br, QW), f32), shape((br, KW), f32), shape((br, KW), f32),
        shape((QW, br), f32), shape((br, F), f32), shape((br, F), f32), shape((F, br), f32),
    )
    outs = pl.pallas_call(
        functools.partial(layer_kernel, plan),
        out_shape=results + (shape((8, D), f32),),
        in_specs=[hbm, whole] + [hbm] * 7 + [whole] * 4 + [hbm],
        out_specs=(hbm,) * 9 + (whole,),
        scratch_shapes=scratch,
        compiler_params=pltpu.CompilerParams(
            collective_id=0, has_side_effects=True, vmem_limit_bytes=64 * 2**20
        ),
        name="layer",
    )(
        tokens, segment_ids, w_query, key_matrix, value_matrix, w_out, w_gate, w_up, w_down,
        norm_attn[None], norm_ffn[None], norm_query[None], norm_key[None], cotangent,
    )
    gain = shape((1, D), f32)
    head_gain = shape((1, norm_query.shape[0]), f32)
    outs = pl.pallas_call(
        hand_out,
        out_shape=results + (gain, gain, head_gain, head_gain),
        in_specs=[pl.BlockSpec(memory_space=pltpu.HBM)] * 9 + [whole],
        out_specs=(pl.BlockSpec(memory_space=pltpu.HBM),) * 9 + (whole,) * 4,
        scratch_shapes=[vm(v.shape, v.dtype) for v in results] + [sem((2, 9))],
        compiler_params=pltpu.CompilerParams(vmem_limit_bytes=63 * 2**20),
        name="hand_out",
    )(*outs)
    return outs[:9] + tuple(v[0] for v in outs[9:])


def solution(mesh):
    in_specs = (
        P("row", "col"), P("row", None), P("row", "col"), P("row", "col"), P("row", "col"), P("col", "row"),
        P("row", "col"), P("row", "col"), P("col", "row"), P(), P(), P(), P(), P("row", "col"),
    )
    out_specs = (
        P("row", "col"), P("row", "col"), P("row", "col"), P("row", "col"), P("row", "col"), P("col", "row"),
        P("row", "col"), P("row", "col"), P("col", "row"), P(), P(), P(), P(),
    )
    return jax.shard_map(
        functools.partial(per_device, mesh.shape["row"]),
        mesh=mesh, in_specs=in_specs, out_specs=out_specs, check_vma=False,
    )
```

time: 240 us -> 187 us (0.78)
  Pallas kernels: 239 us -> 186 us
    pallas_call x1, Pallas kernels: 235 us -> 181 us  [per_device(): pl.pallas_call(functools.partial(layer_kernel, plan), out_shape=results +...]
where the time goes in v3:
time: 187 us
  Pallas kernels  186 us (99%)
    pallas_call x1, Pallas kernels, per_device(): pl.pallas_call(functools.partial(layer_kernel, plan), out_shape=results +...  181 us
    pallas_call x1, Pallas kernels, per_device(): pl.pallas_call(hand_out, out_shape=results + (gain, gain, head_gain, head...  4.59 us

profile of v3, /device:TPU:0, one launch (start us, length us, event | category | flops | bytes accessed | tf_op | source)
XLA Modules:
  0.0 186.8 jit_solution(6253915281436087834)
XLA Ops:
  0.7 181.4 %layer.1 = (bf16[1024,256]{1,0:T(8,128)(2,1)}, f32[1024,256]{1,0:T(8,128)}, f32[128,256]{1,0:T(8,128)}, f32[128,128]{1,0:T(8,128)}, f32[128,128]{1,0:T(8,128)}, ...) custom-call(bf16[1024,256]{1,0:T(8,128)(2,1)} %tok_h.1, ...), custom_call_target="tpu_custom_call" | custom-call | tf_op jit(solution)/shard_map/layer/pallas_call | solution.py:986
  182.1 4.6 %hand_out.1 = (bf16[1024,256]{1,0:T(8,128)(2,1)}, f32[1024,256]{1,0:T(8,128)}, f32[128,256]{1,0:T(8,128)}, f32[128,128]{1,0:T(8,128)}, f32[128,128]{1,0:T(8,128)...) custom-call(bf16[1024,256]{1,0:T(8,128)(2,1)} %get-tuple-element.36., ...), custom_call_target="tpu_custom_call" | custom-call | tf_op jit(solution)/shard_map/hand_out/pallas_call | solution.py:1002
